TPU v7x, 256 devices: a whole 4x4x8 slice. The times are simulated.
256 devices in a mesh: row: 64 (over x, z, core), col: 4 (over y).
Axes of the slice: x: 4, y: 4, z: 8, core: 2. Of those that a mesh axis runs over, the one named last changes fastest.
Arguments:
- matrix: float32 [16384, 16384], P('row', 'col'), as said below
Outputs:
- factored: float32 [16384, 16384], P('row', 'col')
Inputs may be any that keep to these rules, and one draw needn't show every extreme that they name: matrix read in matrix order is symmetric except in its first tile column below the first tile, which holds the panel's factor with entries of order 0.1; diagonal entries lie between 24 and 40, and the tile of updated at rows and columns 128 to 255 is positive definite.
All inputs are finite; a program needn't handle non-finite values.
Results may differ from a plain program's by a relative error of at most 0.00005.
Values sent between devices are 32-bit elements; how exact they have to be, the bound alone decides.
No kernel may reach another device: no remote copies, remote signals or barrier semaphores. Data moves between devices by JAX's collectives and lax.ppermute only.
A program may use at most 64 MiB of HBM per device.

v0:
```python
import jax
import jax.numpy as jnp
from jax import lax
from jax.sharding import PartitionSpec as P

NB = 128


def spread(block, axis, holder):
    block = jnp.where(lax.axis_index(axis) == holder, block, jnp.zeros_like(block))
    return lax.psum(block, axis)


def on_device(matrix):
    rows_here = matrix.shape[0]
    cols_here = matrix.shape[1]
    n_row = lax.axis_size("row")
    n_col = lax.axis_size("col")
    row_index = lax.axis_index("row")
    col_index = lax.axis_index("col")
    tiles_row = rows_here // NB
    received = spread(matrix[:, :NB], "col", 0)
    tile_ids = jnp.arange(rows_here, dtype=jnp.int32) // NB * n_row + row_index
    panel = jnp.where((tile_ids >= 1)[:, None], received, jnp.float32(0.0))
    everything = lax.all_gather(panel, "row", axis=0, tiled=True)
    blocks = everything.reshape(n_row, tiles_row, NB, NB).transpose(1, 0, 2, 3)
    blocks = blocks.reshape(cols_here // NB, n_col, NB, NB)
    matching = lax.dynamic_index_in_dim(blocks, col_index, 1, keepdims=False).reshape(cols_here, NB)
    contract = (((1,), (1,)), ((), ()))
    product = lax.dot_general(
        panel,
        matching,
        contract,
        precision=lax.Precision.HIGHEST,
        preferred_element_type=jnp.float32,
    )
    updated = matrix - product
    pivot = spread(updated[:NB, :NB], "row", 1)
    lower = jnp.linalg.cholesky(pivot)
    column = updated[:, :NB]
    solved = jax.scipy.linalg.solve_triangular(lower, column.T, lower=True).T
    stacked = jnp.tile(lower, (tiles_row, 1))
    fresh = jnp.where(
        (tile_ids >= 2)[:, None], solved, jnp.where((tile_ids == 1)[:, None], stacked, column)
    )
    fresh = jnp.where(col_index == 1, fresh, column)
    return jnp.concatenate([fresh, updated[:, NB:]], axis=1)


def solution(mesh):
    in_specs = (P("row", "col"),)
    out_specs = P("row", "col")
    return jax.shard_map(
        on_device, mesh=mesh, in_specs=in_specs, out_specs=out_specs, check_vma=False
    )
```

profile of v0, /device:TPU:1, one launch (start us, length us, event | category | flops | bytes accessed | tf_op | source)
XLA Modules:
  0.0 362.6 jit_solution(11087832124198132016)
XLA Ops:
  6.5 1.6 slice_select_fusion
  8.1 0.0 all-reduce.3.cloned.1.call-update
  8.1 0.0 all-gather.2.cloned.1.call-start
  8.2 49.5 %all-reduce.3.cloned.1.call-done = f32[256,128]{1,0:T(8,128)} async-done(((f32[256,128]{1,0:T(8,128)}), f32[256,128]{1,0:T(8,128)}) %all-reduce.3.cloned.1.call-update) | async-done | bytes 131088 | tf_op jit(solution)/shard_map/psum | solution.py:11
  57.7 1.7 broadcast_select_fusion
  59.4 0.0 all-reduce.5.cloned.1.call-start
  59.5 87.4 %all-gather.2.cloned.1.call-done = f32[16384,128]{1,0:T(8,128)} async-done(((f32[256,128]{1,0:T(8,128)}), f32[16384,128]{1,0:T(8,128)}) %all-gather.2.cloned.1.call-update) | async-done | bytes 8388624 | tf_op jit(solution)/shard_map/all_gather | solution.py:25
  146.8 4.0 %copy.6 = f32[2,64,128,128]{3,2,1,0:T(8,128)S(1)} copy(f32[2,64,128,128]{3,2,0,1:T(8,128)} %bitcast.19) | data formatting | bytes 16777216 | tf_op jit(solution)/shard_map/transpose | solution.py:26
  150.9 0.1 constant_dynamic-slice_fusion
  151.0 2.0 copy-done.1
  153.0 3.6 convolution_subtract_fusion
  156.7 2.0 copy-done
  158.7 0.6 slice_select_fusion.1
  159.3 4.3 %slice.30 = f32[256,3968]{1,0:T(8,128)} slice(f32[256,4096]{1,0:T(8,128)} %copy-done), slice={[0:256], [128:4096]} | slice | bytes 8126464 | tf_op jit(solution)/shard_map/slice | solution.py:47
  163.7 160.7 %all-reduce.5.cloned.1.call-done = f32[128,128]{1,0:T(8,128)} async-done(((f32[128,128]{1,0:T(8,128)}), f32[128,128]{1,0:T(8,128)}) %all-reduce.5.cloned.1.call-update) | async-done | bytes 65552 | tf_op jit(solution)/shard_map/psum | solution.py:11
  324.4 0.9 copy.7
  325.3 0.9 fusion.3
  326.2 11.7 %cholesky.15 = f32[128,128]{1,0:T(8,128)S(1)} custom-call(f32[128,128]{1,0:T(8,128)S(1)} %fusion.3), custom_call_target="Cholesky" | custom-call | tf_op jit(solution)/shard_map/jit(cholesky)/cholesky | solution.py:39
  337.9 0.7 compare_reduce_fusion
  338.7 0.7 select_bitcast_fusion
  339.3 9.8 %custom-call.7 = f32[1,128,128]{1,2,0:T(8,128)S(1)} custom-call(f32[1,128,128]{2,1,0:T(8,128)S(1)} %get-tuple-element.5), custom_call_target="InvertDiagBlocksLowerTriangular" | custom-call | tf_op jit(solution)/shard_map/jit(_solve_triangular)/triangular_solve | solution.py:41
  349.2 1.0 bitcast_select_fusion
  350.2 1.2 fusion
  351.4 4.6 %pad_maximum_fusion = f32[256,4096]{1,0:T(8,128)} fusion(f32[256,3968]{1,0:T(8,128)} %slice.30, f32[256,128]{1,0:T(8,128)S(1)} %fusion), kind=kLoop, calls=%fused_computation.1 | loop fusion | flops 1048576 | bytes 8388608 | tf_op jit(solution)/shard_map/concatenate | solution.py:47
  (10 shorter events, 0.1 us)
Async XLA Ops:
  6.5 51.2 %all-reduce.3.cloned.1.call-start = ((), (), s32[]{:S(2)}) async-start(), calls=%async_computation | async-start | bytes 262144 | tf_op jit(solution)/shard_map/psum | solution.py:11
  8.1 138.7 %all-gather.2.cloned.1.call-start = ((), (), s32[]{:S(2)}) async-start(), calls=%async_computation.1 | async-start | bytes 8519680 | tf_op jit(solution)/shard_map/all_gather | solution.py:25
  59.4 265.0 %all-reduce.5.cloned.1.call-start = ((), (), s32[]{:S(2)}) async-start(), calls=%async_computation.2 | async-start | bytes 131072 | tf_op jit(solution)/shard_map/psum | solution.py:11
  146.8 4.2 %copy-start.2 = (f32[256,128]{1,0:T(8,128)S(1)}, f32[256,128]{1,0:T(8,128)}, u32[]{:S(2)}) copy-start(f32[256,128]{1,0:T(8,128)} %broadcast_select_fusion) | copy-start | bytes 393220
  150.8 2.2 copy-start.1
  156.6 2.0 copy-start
Sparse Core Ops, SparseCore 0:
  9.7 48.0 all-reduce.2
  60.9 85.9 all-gather.1
  159.4 164.9 all-reduce.4
where the time goes:
time: 363 us
  waiting for transfers between devices  298 us (82%)
  other arithmetic  33.3 us (9%)
  local copies, waits for them, and re-layouts  13.4 us (4%)
  between operations  13.2 us (4%)
  matrix products  4.84 us (1%)
    psum x2, waiting for transfers between devices, spread(): return lax.psum(block, axis)  210 us
    all_gather x1, waiting for transfers between devices, on_device(): everything = lax.all_gather(panel, 'row', axis=0, tiled=True)  87.4 us
    another operation x3, other arithmetic, on_device(): lower = jnp.linalg.cholesky(pivot)  12.5 us
    another operation x2, other arithmetic, on_device(): solved = jax.scipy.linalg.solve_triangular(lower, column.T, lower=True).T  10.5 us
  transfers between devices with their start and end apart: 3, of which 3 were waited for; matrix products, arithmetic and copies ran while one was open for 1% of the time, Pallas kernels for 0%

commit v1 on v0

v1 whole, which is shorter than its diff:
```python
import jax
import jax.numpy as jnp
from jax import lax
from jax.experimental import pallas as pl
from jax.experimental.pallas import tpu as pltpu
from jax.sharding import PartitionSpec as P

NB = 128
NX, NY, NZ, NC = 4, 4, 8, 2
AXES = ("row", "col")
HIGH = lax.Precision.HIGHEST
TRANS = (((1,), (1,)), ((), ()))


def rank(x, y, z, c):
    return ((x * NZ + z) * NC + c) * NY + y


def chips(xs=range(NX), zs=range(NZ), cs=range(NC), ys=range(NY)):
    return [(x, y, z, c) for x in xs for z in zs for c in cs for y in ys]


def shift(block, move, **where):
    pairs = [(rank(*d), rank(*move(*d))) for d in chips(**where)]
    return lax.ppermute(block, AXES, pairs)


def split(v):
    hi = v.astype(jnp.bfloat16)
    lo = (v - hi.astype(jnp.float32)).astype(jnp.bfloat16)
    return hi, lo


def pivot_kernel(a_ref, p_ref, u_ref):
    p = p_ref[...]
    u_ref[...] = a_ref[...] - lax.dot_general(
        p, p, TRANS, precision=HIGH, preferred_element_type=jnp.float32
    )


def factor_kernel(u_ref, low_ref, inv_ref):
    blocks = NB // 8
    lane = lax.broadcasted_iota(jnp.int32, (8, NB), 1)
    sub = lax.broadcasted_iota(jnp.int32, (8, NB), 0)
    s = [u_ref[8 * i : 8 * i + 8, :] for i in range(blocks)]
    t = [(lane == sub + 8 * i).astype(jnp.float32) for i in range(blocks)]
    for j in range(NB):
        b, k = divmod(j, 8)
        row, row_t = s[b][k : k + 1, :], t[b][k : k + 1, :]
        scale = 1.0 / row[:, j : j + 1]
        row, row_t = row * scale, row_t * scale
        for i in range(b, blocks):
            col = jnp.broadcast_to(s[i][:, j : j + 1], (8, NB))
            if i == b:
                col = jnp.where(sub > k, col, 0.0)
            s[i] = s[i] - col * row
            t[i] = t[i] - col * row_t
    upper = []
    for i in range(blocks):
        diag = jnp.sum(jnp.where(lane == sub + 8 * i, s[i], 0.0), axis=1, keepdims=True)
        scale = 1.0 / jnp.sqrt(diag)
        upper.append(jnp.where(lane >= sub + 8 * i, s[i] * scale, 0.0))
        inv_ref[8 * i : 8 * i + 8, :] = t[i] * scale
    low_ref[...] = jnp.concatenate(upper, axis=0).T


def update_kernel(idx_ref, a_ref, p_ref, own_ref, got_ref, low_ref, inv_ref, out_ref, buf, sem):
    x, z, core, y = idx_ref[0], idx_ref[1], idx_ref[2], idx_ref[3]
    row0 = idx_ref[4]
    ph, plo = split(p_ref[...])

    def tile(step, _):
        src = step // 16
        piece = lax.rem(step, 16)
        dx, d = piece // 4, lax.rem(piece, 4)
        level = lax.rem(src + 1 + core, 2)
        m = level * 16 + lax.rem(x + dx, NX) * 4 + (d ^ lax.rem(z, 4))
        rows = pl.ds(pl.multiple_of(piece * NB, NB), NB)
        cols = pl.ds(pl.multiple_of(m * NB, NB), NB)

        def work(ref):
            qh, ql = split(ref[rows, :])
            prod = lax.dot_general(ph, qh, TRANS, preferred_element_type=jnp.float32)
            prod += lax.dot_general(ph, ql, TRANS, preferred_element_type=jnp.float32)
            prod += lax.dot_general(plo, qh, TRANS, preferred_element_type=jnp.float32)
            buf[:, cols] = a_ref[:, cols] - prod

        @pl.when(src == 0)
        def _():
            work(own_ref)

        @pl.when(src == 1)
        def _():
            work(got_ref)

        @pl.when((m == 0) & (y == 1))
        def _():
            column = buf[:, :NB]
            solved = lax.dot_general(
                column, inv_ref[...], TRANS, precision=HIGH, preferred_element_type=jnp.float32
            )
            top, bottom = column[:NB], solved[NB:]
            buf[NB:, :NB] = bottom
            keep = jnp.where(row0 == 1, low_ref[...], solved[:NB])
            buf[:NB, :NB] = jnp.where(row0 == 0, top, keep)

        pltpu.make_async_copy(buf.at[:, cols], out_ref.at[:, cols], sem).start()
        return 0

    lax.fori_loop(0, 32, tile, 0)
    pltpu.make_async_copy(buf, out_ref, sem).wait()


def vmem():
    return pl.BlockSpec(memory_space=pltpu.VMEM)


def smem():
    return pl.BlockSpec(memory_space=pltpu.SMEM)


def on_device(matrix):
    row = lax.axis_index("row")
    y = lax.axis_index("col")
    x, z, core = row // (NZ * NC), row // NC % NZ, row % NC
    tile = jax.ShapeDtypeStruct((NB, NB), jnp.float32)

    panel0 = matrix[:, :NB]
    panel0 = jnp.where((jnp.arange(2 * NB) >= NB)[:, None] | (row > 0), panel0, 0.0)

    first = lax.ppermute(panel0[:NB], AXES, [(rank(0, 0, 0, 1), rank(0, 1, 0, 1))])
    pivot = pl.pallas_call(
        pivot_kernel,
        out_shape=tile,
        grid=(1,),
        in_specs=[
            pl.BlockSpec((NB, NB), lambda i: (0, 0)),
            pl.BlockSpec((NB, NB), lambda i: (0, 0)),
        ],
        out_specs=pl.BlockSpec((NB, NB), lambda i: (0, 0)),
    )(matrix, first)

    piece = jnp.zeros((NB, NB), jnp.float32)
    for a in range(2):
        for c in range(2):
            got = shift(
                panel0[(1 - c) * NB : (2 - c) * NB],
                lambda X, Y, Z, C: (X, 2 * (Z % 2) + C, 4 * a + Z // 2, c),
                ys=[0],
            )
            piece = jnp.where((z // 4 == a) & (core == c), got, piece)

    panel = panel0
    for dy in (1, 3, 2):
        got = shift(panel0, lambda X, Y, Z, C: (X, dy, Z, C), ys=[0])
        panel = jnp.where(y == dy, got, panel)

    parts = [piece] + [
        shift(piece, lambda X, Y, Z, C: (X, Y, Z ^ d, C)) for d in (1, 2, 3)
    ]
    here = jnp.concatenate(parts)

    got = shift(pivot, lambda X, Y, Z, C: (0, 1, 7, 1), xs=[0], ys=[1], zs=[0], cs=[1])
    pivot = jnp.where(z == 7, got, pivot)
    best = pivot
    for d in (1, 2, 3):
        got = shift(pivot, lambda X, Y, Z, C: (X, Y, Z ^ d, C), xs=[0], ys=[1], zs=[0, 7], cs=[1])
        best = jnp.where((z == d) | (z == 7 ^ d), got, best)
    pivot = best
    for dx in (1, 3, 2):
        got = shift(pivot, lambda X, Y, Z, C: (dx, Y, Z, C), xs=[0], ys=[1], cs=[1])
        best = jnp.where(x == dx, got, best)
    pivot = best
    got = shift(pivot, lambda X, Y, Z, C: (X, Y, Z, 0), ys=[1], cs=[1])
    pivot = jnp.where(core == 0, got, pivot)

    left = shift(here, lambda X, Y, Z, C: ((X + 1) % NX, Y, Z, C))
    right = shift(here, lambda X, Y, Z, C: ((X + 3) % NX, Y, Z, C))
    far_a = shift(left[: 2 * NB], lambda X, Y, Z, C: ((X + 1) % NX, Y, Z, C))
    far_b = shift(right[2 * NB :], lambda X, Y, Z, C: ((X + 3) % NX, Y, Z, C))
    own = jnp.concatenate([here, right, far_a, far_b, left])

    other = shift(own, lambda X, Y, Z, C: (X, Y, Z, 1 - C))

    lower, inverse = pl.pallas_call(
        factor_kernel, out_shape=(tile, tile), in_specs=[vmem()], out_specs=(vmem(), vmem())
    )(pivot)

    index = jnp.stack([x, z, core, y, row]).astype(jnp.int32)
    return pl.pallas_call(
        update_kernel,
        out_shape=jax.ShapeDtypeStruct(matrix.shape, jnp.float32),
        in_specs=[smem()] + [vmem()] * 6,
        out_specs=pl.BlockSpec(memory_space=pl.ANY),
        scratch_shapes=[
            pltpu.VMEM(matrix.shape, jnp.float32),
            pltpu.SemaphoreType.DMA,
        ],
        compiler_params=pltpu.CompilerParams(vmem_limit_bytes=32 * 1024 * 1024),
    )(index, matrix, panel, own, other, lower, inverse)


def solution(mesh):
    return jax.shard_map(
        on_device,
        mesh=mesh,
        in_specs=(P("row", "col"),),
        out_specs=P("row", "col"),
        check_vma=False,
    )
```

time: 363 us -> 89.8 us (0.25)
  waiting for transfers between devices: 298 us -> 8.65 us
  starting transfers between devices: 0.09 us -> 48.5 us
  other arithmetic: 33.3 us -> 3.58 us
  Pallas kernels: 0 us -> 23.4 us
  between operations: 13.2 us -> 0.44 us
  local copies, waits for them, and re-layouts: 13.4 us -> 4.69 us
  matrix products: 4.84 us -> 0 us
    psum x2 -> x0, waiting for transfers between devices: 210 us -> none  [spread(): return lax.psum(block, axis)]
    all_gather x1 -> x0, waiting for transfers between devices: 87.4 us -> none  [on_device(): everything = lax.all_gather(panel, 'row', axis=0, tiled=True)]
    ppermute x0 -> x24, starting transfers between devices: none -> 48.5 us  [the longest x23 47.2 us: shift(): return lax.ppermute(block, AXES, pairs)]
    pallas_call x0 -> x3, Pallas kernels: none -> 23.4 us  [the longest x1 12.4 us: on_device(): pl.pallas_call(factor_kernel, out_shape=(tile, tile), in_specs=[vmem()],...]
    another operation x5 -> x0, other arithmetic: 22.9 us -> none  [the longest x3 12.5 us: on_device(): lower = jnp.linalg.cholesky(pivot)]
    ppermute x0 -> x24, waiting for transfers between devices: none -> 8.65 us  [the longest x23 8.65 us: shift(): return lax.ppermute(block, AXES, pairs)]
    concatenate x1, other arithmetic: 4.63 us -> 0.02 us  [on_device(): here = jnp.concatenate(parts)]
    slice x1 -> x3, local copies, waits for them, and re-layouts: 4.33 us -> 0.03 us  [the longest x1 0.01 us: on_device(): panel0[(1 - c) * NB:(2 - c) * NB]]
  transfers between devices with their start and end apart: 3 -> 24, of which waited for: 3 -> 5; matrix products, arithmetic and copies ran while one was open for 1% -> 3% of each run, Pallas kernels for 0% -> 16%
where the time goes in v1:
time: 89.8 us; the launch traced here: 89.2 us
  starting transfers between devices  48.5 us (54%)
  Pallas kernels  23.4 us (26%)
  waiting for transfers between devices  8.65 us (10%)
  local copies, waits for them, and re-layouts  4.69 us (5%)
  other arithmetic  3.58 us (4%)
    ppermute x23, starting transfers between devices, shift(): return lax.ppermute(block, AXES, pairs)  47.2 us
    pallas_call x1, Pallas kernels, on_device(): pl.pallas_call(factor_kernel, out_shape=(tile, tile), in_specs=[vmem()],...  12.4 us
    pallas_call x1, Pallas kernels, on_device(): pl.pallas_call(update_kernel, out_shape=jax.ShapeDtypeStruct(matrix.shape...  9.26 us
    ppermute x23, waiting for transfers between devices, shift(): return lax.ppermute(block, AXES, pairs)  8.65 us
    unnamed x14, local copies, waits for them, and re-layouts  4.56 us
  transfers between devices with their start and end apart: 24, of which 5 were waited for; matrix products, arithmetic and copies ran while one was open for 3% of the time, Pallas kernels for 16%

profile of v1, /device:TPU:1, one launch (start us, length us, event | category | flops | bytes accessed | tf_op | source)
XLA Modules:
  0.0 89.2 jit_solution(18160789662665568030)
XLA Ops:
  0.0 1.0 %slice_select_fusion = f32[256,128]{1,0:T(8,128)S(1)} fusion(f32[256,4096]{1,0:T(8,128)} %a_ref.3, pred[256]{0:T(512)(128)(4,1)S(1)} %compare_or_fusion), kind=kLoop, calls=%fused_computation.2 | loop fusion | flops 32768 | bytes 262400 | tf_op jit(solution)/shard_map/jit(_where)/select_n | solution.py:129
  1.0 4.6 %collective-permute-start.6 = (f32[128,128]{1,0:T(8,128)S(1)}, f32[128,128]{1,0:T(8,128)S(1)}, u32[]{:S(2)}, u32[]{:S(2)}) collective-permute-start(f32[128,128]{1,0:T(8,128)S(1)} %get-tuple-element.11), channel_id=1, source_target_pairs={{0,0},{4,1},{8,2},{12,3},{16,8},{20,9},{24,10},{28,11},{32,16},{36... | collective-permute-start | bytes 196616 | tf_op jit(solution)/shard_map/ppermute | solution.py:25
  5.6 7.3 %collective-permute-start.4 = (f32[128,128]{1,0:T(8,128)S(1)}, f32[128,128]{1,0:T(8,128)S(1)}, u32[]{:S(2)}, u32[]{:S(2)}) collective-permute-start(f32[128,128]{1,0:T(8,128)S(1)} %get-tuple-element.11), channel_id=1, source_target_pairs={{0,32},{4,33},{8,34},{12,35},{16,40},{20,41},{24,42},{28,43},{32,4... | collective-permute-start | bytes 196616 | tf_op jit(solution)/shard_map/ppermute | solution.py:25
  12.9 1.9 %collective-permute-start.5 = (f32[128,128]{1,0:T(8,128)S(1)}, f32[128,128]{1,0:T(8,128)S(1)}, u32[]{:S(2)}, u32[]{:S(2)}) collective-permute-start(f32[128,128]{1,0:T(8,128)S(1)} %get-tuple-element.12), channel_id=1, source_target_pairs={{0,4},{4,5},{8,6},{12,7},{16,12},{20,13},{24,14},{28,15},{32,20},{... | collective-permute-start | bytes 196616 | tf_op jit(solution)/shard_map/ppermute | solution.py:25
  14.9 1.3 %collective-permute-start.3 = (f32[128,128]{1,0:T(8,128)S(1)}, f32[128,128]{1,0:T(8,128)S(1)}, u32[]{:S(2)}, u32[]{:S(2)}) collective-permute-start(f32[128,128]{1,0:T(8,128)S(1)} %get-tuple-element.12), channel_id=1, source_target_pairs={{0,36},{4,37},{8,38},{12,39},{16,44},{20,45},{24,46},{28,47},{32,5... | collective-permute-start | bytes 196616 | tf_op jit(solution)/shard_map/ppermute | solution.py:25
  16.2 1.3 %collective-permute-start.15 = (f32[128,128]{1,0:T(8,128)S(1)}, f32[128,128]{1,0:T(8,128)S(1)}, u32[]{:S(2)}, u32[]{:S(2)}) collective-permute-start(f32[128,128]{1,0:T(8,128)S(1)} %get-tuple-element.12), channel_id=1, source_target_pairs={{4,5}} | collective-permute-start | bytes 196616 | tf_op jit(solution)/shard_map/ppermute | solution.py:131
  17.6 8.2 %collective-permute-start.9 = (f32[128,128]{1,0:T(8,128)S(1)}, f32[128,128]{1,0:T(8,128)S(1)}, u32[]{:S(2)}, u32[]{:S(2)}) collective-permute-start(f32[128,128]{1,0:T(8,128)S(1)} %get-tuple-element.10), channel_id=1, source_target_pairs={{0,24},{1,25},{2,26},{3,27},{4,28},{5,29},{6,30},{7,31},{8,16},{9,... | collective-permute-start | bytes 196616 | tf_op jit(solution)/shard_map/ppermute | solution.py:25
  26.9 1.8 %shard_map.17 = f32[128,128]{1,0:T(8,128)} custom-call(f32[256,4096]{1,0:T(8,128)} %a_ref.3, f32[128,128]{1,0:T(8,128)} %copy-done.3), custom_call_target="tpu_custom_call" | custom-call | tf_op jit(solution)/shard_map/pallas_call | solution.py:132
  29.3 1.5 %collective-permute-done.8 = f32[128,128]{1,0:T(8,128)S(1)} collective-permute-done((f32[128,128]{1,0:T(8,128)S(1)}, f32[128,128]{1,0:T(8,128)S(1)}, u32[]{:S(2)}, u32[]{:S(2)}) %collective-permute-start.8) | collective-permute-done | bytes 65568 | tf_op jit(solution)/shard_map/ppermute | solution.py:25
  30.8 1.3 %collective-permute-start.11 = (f32[512,128]{1,0:T(8,128)S(1)}, f32[512,128]{1,0:T(8,128)S(1)}, u32[]{:S(2)}, u32[]{:S(2)}) collective-permute-start(f32[512,128]{1,0:T(8,128)S(1)} %pad_maximum_fusion), channel_id=1, source_target_pairs={{0,64},{1,65},{2,66},{3,67},{4,68},{5,69},{6,70},{7,71},{8,72},{9,... | collective-permute-start | bytes 786440 | tf_op jit(solution)/shard_map/ppermute | solution.py:25
  35.0 1.5 %collective-permute-start.10 = (f32[512,128]{1,0:T(8,128)S(1)}, f32[512,128]{1,0:T(8,128)S(1)}, u32[]{:S(2)}, u32[]{:S(2)}) collective-permute-start(f32[512,128]{1,0:T(8,128)S(1)} %pad_maximum_fusion), channel_id=1, source_target_pairs={{0,192},{1,193},{2,194},{3,195},{4,196},{5,197},{6,198},{7,199},{8... | collective-permute-start | bytes 786440 | tf_op jit(solution)/shard_map/ppermute | solution.py:25
  36.5 1.5 %collective-permute-done.11 = f32[512,128]{1,0:T(8,128)S(1)} collective-permute-done((f32[512,128]{1,0:T(8,128)S(1)}, f32[512,128]{1,0:T(8,128)S(1)}, u32[]{:S(2)}, u32[]{:S(2)}) %collective-permute-start.11) | collective-permute-done | bytes 262176 | tf_op jit(solution)/shard_map/ppermute | solution.py:25
  38.1 2.5 %collective-permute-done.10 = f32[512,128]{1,0:T(8,128)S(1)} collective-permute-done((f32[512,128]{1,0:T(8,128)S(1)}, f32[512,128]{1,0:T(8,128)S(1)}, u32[]{:S(2)}, u32[]{:S(2)}) %collective-permute-start.10) | collective-permute-done | bytes 262176 | tf_op jit(solution)/shard_map/ppermute | solution.py:25
  40.7 2.8 %collective-permute-start.13 = (f32[256,128]{1,0:T(8,128)S(1)}, f32[256,128]{1,0:T(8,128)S(1)}, u32[]{:S(2)}, u32[]{:S(2)}) collective-permute-start(f32[256,128]{1,0:T(8,128)S(1)} %slice.26), channel_id=1, source_target_pairs={{0,192},{1,193},{2,194},{3,195},{4,196},{5,197},{6,198},{7,199},{8... | collective-permute-start | bytes 393224 | tf_op jit(solution)/shard_map/ppermute | solution.py:25
  43.5 1.9 %collective-permute-done.13 = f32[256,128]{1,0:T(8,128)S(1)} collective-permute-done((f32[256,128]{1,0:T(8,128)S(1)}, f32[256,128]{1,0:T(8,128)S(1)}, u32[]{:S(2)}, u32[]{:S(2)}) %collective-permute-start.13) | collective-permute-done | bytes 131104 | tf_op jit(solution)/shard_map/ppermute | solution.py:25
  45.4 4.0 %collective-permute-start.14 = (f32[2048,128]{1,0:T(8,128)S(1)}, f32[2048,128]{1,0:T(8,128)S(1)}, u32[]{:S(2)}, u32[]{:S(2)}) collective-permute-start(f32[2048,128]{1,0:T(8,128)S(1)} %constant_dynamic-update-slice_fusion.own_ref), channel_id=1, source_target_pairs={{0,4},{1,5},{2,6},{3,7},{4,0},{5,1},{6,2},{7,3},{8,12},{9,13},{10,... | collective-permute-start | bytes 3145736 | tf_op jit(solution)/shard_map/ppermute | solution.py:25
  51.5 5.9 %collective-permute-start.2 = (f32[256,128]{1,0:T(8,128)S(1)}, f32[256,128]{1,0:T(8,128)S(1)}, u32[]{:S(2)}, u32[]{:S(2)}) collective-permute-start(f32[256,128]{1,0:T(8,128)S(1)} %slice_select_fusion), channel_id=1, source_target_pairs={{0,1},{4,5},{8,9},{12,13},{16,17},{20,21},{24,25},{28,29},{32,33},... | collective-permute-start | bytes 393224 | tf_op jit(solution)/shard_map/ppermute | solution.py:25
  57.5 1.3 %collective-permute-start.1 = (f32[256,128]{1,0:T(8,128)S(1)}, f32[256,128]{1,0:T(8,128)S(1)}, u32[]{:S(2)}, u32[]{:S(2)}) collective-permute-start(f32[256,128]{1,0:T(8,128)S(1)} %slice_select_fusion), channel_id=1, source_target_pairs={{0,3},{4,7},{8,11},{12,15},{16,19},{20,23},{24,27},{28,31},{32,35}... | collective-permute-start | bytes 393224 | tf_op jit(solution)/shard_map/ppermute | solution.py:25
  58.8 1.3 %collective-permute-start = (f32[256,128]{1,0:T(8,128)S(1)}, f32[256,128]{1,0:T(8,128)S(1)}, u32[]{:S(2)}, u32[]{:S(2)}) collective-permute-start(f32[256,128]{1,0:T(8,128)S(1)} %slice_select_fusion), channel_id=1, source_target_pairs={{0,2},{4,6},{8,10},{12,14},{16,18},{20,22},{24,26},{28,30},{32,34}... | collective-permute-start | bytes 393224 | tf_op jit(solution)/shard_map/ppermute | solution.py:25
  60.9 1.2 %collective-permute-done = f32[256,128]{1,0:T(8,128)S(1)} collective-permute-done((f32[256,128]{1,0:T(8,128)S(1)}, f32[256,128]{1,0:T(8,128)S(1)}, u32[]{:S(2)}, u32[]{:S(2)}) %collective-permute-start) | collective-permute-done | bytes 131104 | tf_op jit(solution)/shard_map/ppermute | solution.py:25
  62.1 1.0 %select_select_fusion.p_ref = f32[256,128]{1,0:T(8,128)S(1)} fusion(f32[256,128]{1,0:T(8,128)S(1)} %collective-permute-done, f32[256,128]{1,0:T(8,128)S(1)} %collective-permute-done.1, f32[256,128]{1,0:T(8,128)S(1)} %collective-permute-done.2, pred[]{:T(512)S(6)} %eq.61, pred[]{:T(512)S(6)} %eq.60, pred[]{:T(512)S(6)} %eq.59, f32[256,4096]{1,0:T(8,128)} %a_ref.3, ...), kind=kLoop, calls=%fused_computation.1 | loop fusion | flops 131072 | bytes 655619 | tf_op jit(solution)/shard_map/jit(_where)/select_n | solution.py:156
  63.7 12.4 %shard_map.18 = (f32[128,128]{1,0:T(8,128)}, f32[128,128]{1,0:T(8,128)}) custom-call(f32[128,128]{1,0:T(8,128)} %broadcast_select_fusion.1.u_ref), custom_call_target="tpu_custom_call" | custom-call | tf_op jit(solution)/shard_map/pallas_call | solution.py:185
  76.1 2.2 %copy-done = f32[256,4096]{1,0:T(8,128)S(1)} copy-done((f32[256,4096]{1,0:T(8,128)S(1)}, f32[256,4096]{1,0:T(8,128)}, u32[]{:S(2)}) %copy-start) | copy-done | bytes 4194328
  80.0 9.3 %shard_map.19 = f32[256,4096]{1,0:T(8,128)} custom-call(s32[5]{0:T(128)S(1)} %stack.23.idx_ref, f32[256,4096]{1,0:T(8,128)S(1)} %copy-done, f32[256,128]{1,0:T(8,128)S(1)} %select_select_fusion.p_ref, f32[2048,128]{1,0:T(8,128)S(1)} %constant_dynamic-update-slice_fusion.own_ref, f32[2048,128]{1,0:T(8,128)S(1)} %collective-permute-done.14.got_ref, ...), custom_call_target="tpu_custom_call" | custom-call | tf_op jit(solution)/shard_map/pallas_call | solution.py:190
  (55 shorter events, 9.9 us)
Async XLA Ops:
  1.0 16.5 %collective-permute-start.6 = (f32[128,128]{1,0:T(8,128)S(1)}, f32[128,128]{1,0:T(8,128)S(1)}, u32[]{:S(2)}, u32[]{:S(2)}) collective-permute-start(f32[128,128]{1,0:T(8,128)S(1)} %get-tuple-element.11), channel_id=1, source_target_pairs={{0,0},{4,1},{8,2},{12,3},{16,8},{20,9},{24,10},{28,11},{32,16},{36... | collective-permute-start | bytes 196616 | tf_op jit(solution)/shard_map/ppermute | solution.py:25
  5.6 11.9 %collective-permute-start.4 = (f32[128,128]{1,0:T(8,128)S(1)}, f32[128,128]{1,0:T(8,128)S(1)}, u32[]{:S(2)}, u32[]{:S(2)}) collective-permute-start(f32[128,128]{1,0:T(8,128)S(1)} %get-tuple-element.11), channel_id=1, source_target_pairs={{0,32},{4,33},{8,34},{12,35},{16,40},{20,41},{24,42},{28,43},{32,4... | collective-permute-start | bytes 196616 | tf_op jit(solution)/shard_map/ppermute | solution.py:25
  12.9 4.6 %collective-permute-start.5 = (f32[128,128]{1,0:T(8,128)S(1)}, f32[128,128]{1,0:T(8,128)S(1)}, u32[]{:S(2)}, u32[]{:S(2)}) collective-permute-start(f32[128,128]{1,0:T(8,128)S(1)} %get-tuple-element.12), channel_id=1, source_target_pairs={{0,4},{4,5},{8,6},{12,7},{16,12},{20,13},{24,14},{28,15},{32,20},{... | collective-permute-start | bytes 196616 | tf_op jit(solution)/shard_map/ppermute | solution.py:25
  14.9 2.7 %collective-permute-start.3 = (f32[128,128]{1,0:T(8,128)S(1)}, f32[128,128]{1,0:T(8,128)S(1)}, u32[]{:S(2)}, u32[]{:S(2)}) collective-permute-start(f32[128,128]{1,0:T(8,128)S(1)} %get-tuple-element.12), channel_id=1, source_target_pairs={{0,36},{4,37},{8,38},{12,39},{16,44},{20,45},{24,46},{28,47},{32,5... | collective-permute-start | bytes 196616 | tf_op jit(solution)/shard_map/ppermute | solution.py:25
  16.2 10.1 %collective-permute-start.15 = (f32[128,128]{1,0:T(8,128)S(1)}, f32[128,128]{1,0:T(8,128)S(1)}, u32[]{:S(2)}, u32[]{:S(2)}) collective-permute-start(f32[128,128]{1,0:T(8,128)S(1)} %get-tuple-element.12), channel_id=1, source_target_pairs={{4,5}} | collective-permute-start | bytes 196616 | tf_op jit(solution)/shard_map/ppermute | solution.py:131
  17.6 11.7 %collective-permute-start.9 = (f32[128,128]{1,0:T(8,128)S(1)}, f32[128,128]{1,0:T(8,128)S(1)}, u32[]{:S(2)}, u32[]{:S(2)}) collective-permute-start(f32[128,128]{1,0:T(8,128)S(1)} %get-tuple-element.10), channel_id=1, source_target_pairs={{0,24},{1,25},{2,26},{3,27},{4,28},{5,29},{6,30},{7,31},{8,16},{9,... | collective-permute-start | bytes 196616 | tf_op jit(solution)/shard_map/ppermute | solution.py:25
  25.8 4.9 %collective-permute-start.8 = (f32[128,128]{1,0:T(8,128)S(1)}, f32[128,128]{1,0:T(8,128)S(1)}, u32[]{:S(2)}, u32[]{:S(2)}) collective-permute-start(f32[128,128]{1,0:T(8,128)S(1)} %get-tuple-element.10), channel_id=1, source_target_pairs={{0,16},{1,17},{2,18},{3,19},{4,20},{5,21},{6,22},{7,23},{8,24},{9,... | collective-permute-start | bytes 196616 | tf_op jit(solution)/shard_map/ppermute | solution.py:25
  25.9 4.9 %collective-permute-start.7 = (f32[128,128]{1,0:T(8,128)S(1)}, f32[128,128]{1,0:T(8,128)S(1)}, u32[]{:S(2)}, u32[]{:S(2)}) collective-permute-start(f32[128,128]{1,0:T(8,128)S(1)} %get-tuple-element.10), channel_id=1, source_target_pairs={{0,8},{1,9},{2,10},{3,11},{4,12},{5,13},{6,14},{7,15},{8,0},{9,1},... | collective-permute-start | bytes 196616 | tf_op jit(solution)/shard_map/ppermute | solution.py:25
  28.6 3.5 %collective-permute-start.16 = (f32[128,128]{1,0:T(8,128)}, f32[128,128]{1,0:T(8,128)S(1)}, u32[]{:S(2)}, u32[]{:S(2)}) collective-permute-start(f32[128,128]{1,0:T(8,128)} %shard_map.17), channel_id=1, source_target_pairs={{5,61}} | collective-permute-start | bytes 196616 | tf_op jit(solution)/shard_map/ppermute | solution.py:25
  30.8 7.2 %collective-permute-start.11 = (f32[512,128]{1,0:T(8,128)S(1)}, f32[512,128]{1,0:T(8,128)S(1)}, u32[]{:S(2)}, u32[]{:S(2)}) collective-permute-start(f32[512,128]{1,0:T(8,128)S(1)} %pad_maximum_fusion), channel_id=1, source_target_pairs={{0,64},{1,65},{2,66},{3,67},{4,68},{5,69},{6,70},{7,71},{8,72},{9,... | collective-permute-start | bytes 786440 | tf_op jit(solution)/shard_map/ppermute | solution.py:25
  32.9 16.5 %collective-permute-start.19 = (f32[128,128]{1,0:T(8,128)S(1)}, f32[128,128]{1,0:T(8,128)S(1)}, u32[]{:S(2)}, u32[]{:S(2)}) collective-permute-start(f32[128,128]{1,0:T(8,128)S(1)} %broadcast_select_fusion), channel_id=1, source_target_pairs={{5,13},{61,53}} | collective-permute-start | bytes 196616 | tf_op jit(solution)/shard_map/ppermute | solution.py:25
  33.6 15.8 %collective-permute-start.18 = (f32[128,128]{1,0:T(8,128)S(1)}, f32[128,128]{1,0:T(8,128)S(1)}, u32[]{:S(2)}, u32[]{:S(2)}) collective-permute-start(f32[128,128]{1,0:T(8,128)S(1)} %broadcast_select_fusion), channel_id=1, source_target_pairs={{5,21},{61,45}} | collective-permute-start | bytes 196616 | tf_op jit(solution)/shard_map/ppermute | solution.py:25
  34.3 15.2 %collective-permute-start.17 = (f32[128,128]{1,0:T(8,128)S(1)}, f32[128,128]{1,0:T(8,128)S(1)}, u32[]{:S(2)}, u32[]{:S(2)}) collective-permute-start(f32[128,128]{1,0:T(8,128)S(1)} %broadcast_select_fusion), channel_id=1, source_target_pairs={{5,29},{61,37}} | collective-permute-start | bytes 196616 | tf_op jit(solution)/shard_map/ppermute | solution.py:25
  35.0 5.7 %collective-permute-start.10 = (f32[512,128]{1,0:T(8,128)S(1)}, f32[512,128]{1,0:T(8,128)S(1)}, u32[]{:S(2)}, u32[]{:S(2)}) collective-permute-start(f32[512,128]{1,0:T(8,128)S(1)} %pad_maximum_fusion), channel_id=1, source_target_pairs={{0,192},{1,193},{2,194},{3,195},{4,196},{5,197},{6,198},{7,199},{8... | collective-permute-start | bytes 786440 | tf_op jit(solution)/shard_map/ppermute | solution.py:25
  38.0 5.4 %collective-permute-start.12 = (f32[256,128]{1,0:T(8,128)S(1)}, f32[256,128]{1,0:T(8,128)S(1)}, u32[]{:S(2)}, u32[]{:S(2)}) collective-permute-start(f32[256,128]{1,0:T(8,128)S(1)} %slice.25), channel_id=1, source_target_pairs={{0,64},{1,65},{2,66},{3,67},{4,68},{5,69},{6,70},{7,71},{8,72},{9,... | collective-permute-start | bytes 393224 | tf_op jit(solution)/shard_map/ppermute | solution.py:25
  40.7 4.7 %collective-permute-start.13 = (f32[256,128]{1,0:T(8,128)S(1)}, f32[256,128]{1,0:T(8,128)S(1)}, u32[]{:S(2)}, u32[]{:S(2)}) collective-permute-start(f32[256,128]{1,0:T(8,128)S(1)} %slice.26), channel_id=1, source_target_pairs={{0,192},{1,193},{2,194},{3,195},{4,196},{5,197},{6,198},{7,199},{8... | collective-permute-start | bytes 393224 | tf_op jit(solution)/shard_map/ppermute | solution.py:25
  45.4 30.7 %collective-permute-start.14 = (f32[2048,128]{1,0:T(8,128)S(1)}, f32[2048,128]{1,0:T(8,128)S(1)}, u32[]{:S(2)}, u32[]{:S(2)}) collective-permute-start(f32[2048,128]{1,0:T(8,128)S(1)} %constant_dynamic-update-slice_fusion.own_ref), channel_id=1, source_target_pairs={{0,4},{1,5},{2,6},{3,7},{4,0},{5,1},{6,2},{7,3},{8,12},{9,13},{10,... | collective-permute-start | bytes 3145736 | tf_op jit(solution)/shard_map/ppermute | solution.py:25
  49.5 8.0 %collective-permute-start.22 = (f32[128,128]{1,0:T(8,128)S(1)}, f32[128,128]{1,0:T(8,128)S(1)}, u32[]{:S(2)}, u32[]{:S(2)}) collective-permute-start(f32[128,128]{1,0:T(8,128)S(1)} %select_select_fusion.2), channel_id=1, source_target_pairs={{5,69},{13,77},{21,85},{29,93},{37,101},{45,109},{53,117},{61,125}} | collective-permute-start | bytes 196616 | tf_op jit(solution)/shard_map/ppermute | solution.py:25
  50.2 8.7 %collective-permute-start.21 = (f32[128,128]{1,0:T(8,128)S(1)}, f32[128,128]{1,0:T(8,128)S(1)}, u32[]{:S(2)}, u32[]{:S(2)}) collective-permute-start(f32[128,128]{1,0:T(8,128)S(1)} %select_select_fusion.2), channel_id=1, source_target_pairs={{5,197},{13,205},{21,213},{29,221},{37,229},{45,237},{53,245},{61,... | collective-permute-start | bytes 196616 | tf_op jit(solution)/shard_map/ppermute | solution.py:25
  50.8 9.3 %collective-permute-start.20 = (f32[128,128]{1,0:T(8,128)S(1)}, f32[128,128]{1,0:T(8,128)S(1)}, u32[]{:S(2)}, u32[]{:S(2)}) collective-permute-start(f32[128,128]{1,0:T(8,128)S(1)} %select_select_fusion.2), channel_id=1, source_target_pairs={{5,133},{13,141},{21,149},{29,157},{37,165},{45,173},{53,181},{61,... | collective-permute-start | bytes 196616 | tf_op jit(solution)/shard_map/ppermute | solution.py:25
  51.5 9.4 %collective-permute-start.2 = (f32[256,128]{1,0:T(8,128)S(1)}, f32[256,128]{1,0:T(8,128)S(1)}, u32[]{:S(2)}, u32[]{:S(2)}) collective-permute-start(f32[256,128]{1,0:T(8,128)S(1)} %slice_select_fusion), channel_id=1, source_target_pairs={{0,1},{4,5},{8,9},{12,13},{16,17},{20,21},{24,25},{28,29},{32,33},... | collective-permute-start | bytes 393224 | tf_op jit(solution)/shard_map/ppermute | solution.py:25
  57.5 3.3 %collective-permute-start.1 = (f32[256,128]{1,0:T(8,128)S(1)}, f32[256,128]{1,0:T(8,128)S(1)}, u32[]{:S(2)}, u32[]{:S(2)}) collective-permute-start(f32[256,128]{1,0:T(8,128)S(1)} %slice_select_fusion), channel_id=1, source_target_pairs={{0,3},{4,7},{8,11},{12,15},{16,19},{20,23},{24,27},{28,31},{32,35}... | collective-permute-start | bytes 393224 | tf_op jit(solution)/shard_map/ppermute | solution.py:25
  58.8 3.2 %collective-permute-start = (f32[256,128]{1,0:T(8,128)S(1)}, f32[256,128]{1,0:T(8,128)S(1)}, u32[]{:S(2)}, u32[]{:S(2)}) collective-permute-start(f32[256,128]{1,0:T(8,128)S(1)} %slice_select_fusion), channel_id=1, source_target_pairs={{0,2},{4,6},{8,10},{12,14},{16,18},{20,22},{24,26},{28,30},{32,34}... | collective-permute-start | bytes 393224 | tf_op jit(solution)/shard_map/ppermute | solution.py:25
  60.2 2.9 %collective-permute-start.23 = (f32[128,128]{1,0:T(8,128)S(1)}, f32[128,128]{1,0:T(8,128)S(1)}, u32[]{:S(2)}, u32[]{:S(2)}) collective-permute-start(f32[128,128]{1,0:T(8,128)S(1)} %select_select_fusion.1), channel_id=1, source_target_pairs={{5,1},{13,9},{21,17},{29,25},{37,33},{45,41},{53,49},{61,57},{69,6... | collective-permute-start | bytes 196616 | tf_op jit(solution)/shard_map/ppermute | solution.py:25
  (4 other events, 4.5 us)

commit v2 on v0

v2 whole, which is shorter than its diff:
```python
import jax
import jax.numpy as jnp
from jax import lax
from jax.experimental import pallas as pl
from jax.experimental.pallas import tpu as pltpu
from jax.sharding import PartitionSpec as P

NB = 128
NX, NY, NZ, NC = 4, 4, 8, 2
AXES = ("row", "col")
HIGH = lax.Precision.HIGHEST
TRANS = (((1,), (1,)), ((), ()))
MIB = 1024 * 1024


def rank(x, y, z, c):
    return ((x * NZ + z) * NC + c) * NY + y


def move(block, to, where=lambda x, y, z, c: True):
    pairs = [
        (rank(x, y, z, c), rank(*to(x, y, z, c)))
        for x in range(NX)
        for z in range(NZ)
        for c in range(NC)
        for y in range(NY)
        if where(x, y, z, c)
    ]
    return lax.ppermute(block, AXES, pairs)


def split(v):
    hi = v.astype(jnp.bfloat16)
    lo = (v - hi.astype(jnp.float32)).astype(jnp.bfloat16)
    return hi, lo


def times_transposed(left_hi, left_both, right):
    hi, lo = split(right)
    both = lax.dot_general(
        left_both, jnp.concatenate([hi, hi], axis=1), TRANS, preferred_element_type=jnp.float32
    )
    return both + lax.dot_general(left_hi, lo, TRANS, preferred_element_type=jnp.float32)


def factor_kernel(a_ref, p_ref, low_ref, inv_ref, u_ref):
    p = p_ref[...]
    u_ref[...] = a_ref[...] - lax.dot_general(
        p, p, TRANS, precision=HIGH, preferred_element_type=jnp.float32
    )
    n = NB // 8
    lane = lax.broadcasted_iota(jnp.int32, (8, NB), 1)
    sub = lax.broadcasted_iota(jnp.int32, (8, NB), 0)
    s = [u_ref[8 * i : 8 * i + 8, :] for i in range(n)]
    t = [(lane == sub + 8 * i).astype(jnp.float32) for i in range(n)]

    def spread(v, k):
        return jnp.broadcast_to(v[k : k + 1, :], (8, NB))

    for b in range(n):
        cols = [
            [jnp.broadcast_to(s[i][:, 8 * b + k : 8 * b + k + 1], (8, NB)) for i in range(b, n)]
            for k in range(8)
        ]
        factors = []
        for k in range(8):
            inv = 1.0 / spread(cols[k][0], k)
            f = [c * inv for c in cols[k]]
            f[0] = jnp.where(sub > k, f[0], 0.0)
            factors.append(f)
            for m in range(k + 1, 8):
                e = spread(cols[m][0], k)
                cols[m] = [c - g * e for c, g in zip(cols[m], f)]
            r, q = spread(s[b], k), spread(t[b], k)
            s[b] = s[b] - f[0] * r
            t[b] = t[b] - f[0] * q
        for k in range(8):
            r, q = spread(s[b], k), spread(t[b], k)
            for i in range(1, n - b):
                s[b + i] = s[b + i] - factors[k][i] * r
                t[b + i] = t[b + i] - factors[k][i] * q
    upper = []
    for i in range(n):
        diag = jnp.sum(jnp.where(lane == sub + 8 * i, s[i], 0.0), axis=1, keepdims=True)
        scale = 1.0 / jnp.sqrt(diag)
        upper.append(jnp.where(lane >= sub + 8 * i, s[i] * scale, 0.0))
        inv_ref[8 * i : 8 * i + 8, :] = t[i] * scale
    low_ref[...] = jnp.concatenate(upper, axis=0).T


def place():
    row = lax.axis_index("row")
    return row // (NZ * NC), row // NC % NZ, row % NC, lax.axis_index("col"), row


def panels(y, p_ref):
    p = jnp.where(y == 0, p_ref[0][...], jnp.where(y == 1, p_ref[1][...], p_ref[2][...]))
    hi, lo = split(p)
    return hi, jnp.concatenate([hi, lo], axis=1)


def update_kernel(hops, last, a_ref, *refs):
    p_refs, refs = refs[:3], refs[3:]
    count = 8 if last else 2 * len(hops)
    pieces, refs = refs[:count], refs[count:]
    if last:
        low_ref, inv_ref, refs = refs[0], refs[1], refs[2:]
    if hops[0] != 0:
        refs = refs[1:]
    out_ref, a_buf, o_buf, in_sem, out_sem = refs[:5]
    x, z, core, y, row = place()
    even = z % 2 == y // 2
    slots = [jnp.where(even ^ (d % 2 == 1), z ^ d, 7 - (z ^ d)) // 2 for d in (0, 2, 1, 3)]
    groups = [(e, s) for e in hops for s in range(2)]

    def start_of(e, s):
        level = lax.rem(s + 1 + core, 2)
        return (level * 4 + (x ^ e)) * 4 * NB

    ins = []
    for i, (e, s) in enumerate(groups):
        cols = pl.ds(pl.multiple_of(start_of(e, s), 4 * NB), 4 * NB)
        ins.append(pltpu.make_async_copy(a_ref.at[:, cols], a_buf.at[i], in_sem.at[i]))
        ins[-1].start()
    if last:
        col_buf, res_buf, piece_buf, col_sem, res_sem = refs[5:]
        col_in = pltpu.make_async_copy(a_ref.at[:, :NB], col_buf, col_sem)
        col_in.start()
    hi, both = panels(y, p_refs)

    special = y == 1
    if last:
        for e in range(4):
            for s in range(2):
                for d in range(4):

                    @pl.when((x == e) & (core == 1 - s) & (slots[d] == 0))
                    def _():
                        piece_buf[...] = pieces[2 * e + s][d * NB : (d + 1) * NB, :]

        col_in.wait()

        @pl.when(special)
        def _():
            column = col_buf[...] - times_transposed(hi, both, piece_buf[...])
            solved = lax.dot_general(
                column, inv_ref[...], TRANS, precision=HIGH, preferred_element_type=jnp.float32
            )
            res_buf[NB:, :] = solved[NB:]
            keep = jnp.where(row == 1, low_ref[...], solved[:NB])
            res_buf[:NB, :] = jnp.where(row == 0, column[:NB], keep)
            pltpu.make_async_copy(res_buf, out_ref.at[:, :NB], res_sem).start()

    outs = []
    for i, (e, s) in enumerate(groups):
        ref = pieces[2 * e + s] if last else pieces[i]
        prod = times_transposed(hi, both, ref[...])
        ins[i].wait()
        for d in range(4):
            cols = pl.ds(pl.multiple_of(slots[d] * NB, NB), NB)
            o_buf[i, :, cols] = a_buf[i, :, cols] - prod[:, d * NB : (d + 1) * NB]
        begin = start_of(e, s)
        for d in range(4):
            cols = pl.ds(pl.multiple_of(begin + d * NB, NB), NB)
            copy = pltpu.make_async_copy(
                o_buf.at[i, :, d * NB : (d + 1) * NB], out_ref.at[:, cols], out_sem.at[i, d]
            )
            write = jnp.logical_not(special & (begin + d * NB == 0)) if last else None
            outs.append((copy, write))
            if write is None:
                copy.start()
            else:
                pl.when(write)(copy.start)
    for copy, write in outs:
        if write is None:
            copy.wait()
        else:
            pl.when(write)(copy.wait)
    if last:

        @pl.when(special)
        def _():
            pltpu.make_async_copy(res_buf, out_ref.at[:, :NB], res_sem).wait()


def vmem():
    return pl.BlockSpec(memory_space=pltpu.VMEM)


def update(hops, matrix, cands, pieces, out=None, factors=()):
    last = len(factors) > 0
    groups = 2 * len(hops)
    hbm = pl.BlockSpec(memory_space=pltpu.HBM)
    args = [matrix, *cands, *pieces, *factors]
    specs = [hbm] + [vmem()] * (len(args) - 1)
    alias = {}
    if out is not None:
        alias = {len(args): 0}
        args.append(out)
        specs.append(hbm)
    scratch = [
        pltpu.VMEM((groups, 2 * NB, 4 * NB), jnp.float32),
        pltpu.VMEM((groups, 2 * NB, 4 * NB), jnp.float32),
        pltpu.SemaphoreType.DMA((groups,)),
        pltpu.SemaphoreType.DMA((groups, 4)),
    ]
    if last:
        scratch += [
            pltpu.VMEM((2 * NB, NB), jnp.float32),
            pltpu.VMEM((2 * NB, NB), jnp.float32),
            pltpu.VMEM((NB, NB), jnp.float32),
            pltpu.SemaphoreType.DMA,
            pltpu.SemaphoreType.DMA,
        ]

    def kernel(*refs):
        update_kernel(hops, last, *refs)

    return pl.pallas_call(
        kernel,
        out_shape=jax.ShapeDtypeStruct(matrix.shape, jnp.float32),
        in_specs=specs,
        out_specs=hbm,
        scratch_shapes=scratch,
        input_output_aliases=alias,
        compiler_params=pltpu.CompilerParams(vmem_limit_bytes=16 * MIB),
        cost_estimate=pl.CostEstimate(
            flops=groups * 2 * NB * NB * 4 * NB * 8,
            bytes_accessed=groups * 2 * NB * 4 * NB * 8,
            transcendentals=0,
        ),
    )(*args)


def on_device(matrix):
    x, z, core, y, row = place()
    tile = jax.ShapeDtypeStruct((NB, NB), jnp.float32)

    panel = matrix[:, :NB]
    panel = jnp.where((jnp.arange(2 * NB) >= NB)[:, None] | (row > 0), panel, 0.0)

    plane = lambda X, Y, Z, C: 2 * (Z % 2) + C
    source = lambda X, Y, Z, C: Y == 0
    got_a = move(panel[:NB], lambda X, Y, Z, C: (X, plane(X, Y, Z, C), Z, 1), source)
    got_b = move(panel[NB:], lambda X, Y, Z, C: (X, plane(X, Y, Z, C), Z, 0), source)
    piece = jnp.where(core == 1, got_a, got_b)

    rows_a = move(panel, lambda X, Y, Z, C: (X, Y ^ 1, Z, C))
    piece, rows_a = lax.optimization_barrier((piece, rows_a))
    rows_b = move(
        jnp.where(y == 1, rows_a, panel), lambda X, Y, Z, C: (X, Y ^ 3, Z, C)
    )

    tile_of = lambda X, Y, Z, C: Y < 2 and (X, Z, C) == (0, 0, 1)
    seed, piece = lax.optimization_barrier((panel[:NB], piece))
    got = move(seed, lambda X, Y, Z, C: (X, Y, 7, C), tile_of)
    seed = jnp.where(z == 7, got, seed)
    got = move(
        seed,
        lambda X, Y, Z, C: (X, Y, Z ^ 2, C),
        lambda X, Y, Z, C: Y < 2 and X == 0 and C == 1 and Z in (0, 7),
    )
    seed = jnp.where((z == 2) | (z == 5), got, seed)
    got = move(
        seed,
        lambda X, Y, Z, C: (X, Y, Z ^ 1, C),
        lambda X, Y, Z, C: Y < 2 and X == 0 and C == 1 and Z in (0, 2, 5, 7),
    )
    seed = jnp.where((z == 1) | (z == 3) | (z == 4) | (z == 6), got, seed)
    got = move(
        seed,
        lambda X, Y, Z, C: (2, Y, Z, C),
        lambda X, Y, Z, C: Y < 2 and X == 0 and C == 1,
    )
    seed = jnp.where(x == 2, got, seed)
    got = move(
        seed,
        lambda X, Y, Z, C: (X + 1, Y, Z, C),
        lambda X, Y, Z, C: Y < 2 and X in (0, 2) and C == 1,
    )
    seed = jnp.where((x == 1) | (x == 3), got, seed)
    got = move(seed, lambda X, Y, Z, C: (X, Y, Z, 0), lambda X, Y, Z, C: Y < 2 and C == 1)
    seed = jnp.where(core == 0, got, seed)
    pivot_rows = move(seed, lambda X, Y, Z, C: (X, 1, Z, C), lambda X, Y, Z, C: Y == 0)

    holds = lambda X, Y, Z, C: Z % 2 == Y // 2
    mirrored = move(piece, lambda X, Y, Z, C: (X, Y, 7 - Z, C), holds)
    piece = jnp.where(z % 2 == y // 2, piece, mirrored)

    two = jnp.concatenate([piece, move(piece, lambda X, Y, Z, C: (X, Y, Z ^ 2, C))])
    two, rows_b = lax.optimization_barrier((two, rows_b))
    cands = [panel, rows_a, rows_b]
    four = jnp.concatenate([two, move(two, lambda X, Y, Z, C: (X, Y, Z ^ 1, C))])

    factors = pl.pallas_call(
        factor_kernel,
        out_shape=(tile, tile),
        in_specs=[vmem(), vmem()],
        out_specs=(vmem(), vmem()),
        scratch_shapes=[pltpu.VMEM((NB, NB), jnp.float32)],
        compiler_params=pltpu.CompilerParams(vmem_limit_bytes=8 * MIB),
        cost_estimate=pl.CostEstimate(
            flops=6 * 10**9, bytes_accessed=3 * NB * NB * 4, transcendentals=0
        ),
    )(seed, pivot_rows)

    other = lambda X, Y, Z, C: (X, Y, Z, 1 - C)
    near_a = move(four, lambda X, Y, Z, C: (X ^ 1, Y, Z, C))
    near_b = move(four, lambda X, Y, Z, C: (X ^ 3, Y, Z, C))
    four_o = move(four, other)
    far = jnp.concatenate(
        [
            move(near_b[: 2 * NB], lambda X, Y, Z, C: (X ^ 1, Y, Z, C)),
            move(near_a[2 * NB :], lambda X, Y, Z, C: (X ^ 3, Y, Z, C)),
        ]
    )
    near_a_o, near_b_o = move(near_a, other), move(near_b, other)
    far, factors = lax.optimization_barrier((far, factors))
    far_o = move(far, other)

    out = update((0,), matrix, cands, [four, four_o])
    out = update((1, 3), matrix, cands, [near_a, near_a_o, near_b, near_b_o], out)
    pieces = [four, four_o, near_a, near_a_o, far, far_o, near_b, near_b_o]
    return update((2,), matrix, cands, pieces, out, factors)


def solution(mesh):
    return jax.shard_map(
        on_device,
        mesh=mesh,
        in_specs=(P("row", "col"),),
        out_specs=P("row", "col"),
        check_vma=False,
    )
```

time: 363 us -> 62.2 us (0.17)
  waiting for transfers between devices: 298 us -> 10.8 us
  starting transfers between devices: 0.09 us -> 37.6 us
  other arithmetic: 33.3 us -> 2.12 us
  local copies, waits for them, and re-layouts: 13.4 us -> 0.06 us
  between operations: 13.2 us -> 0.58 us
  Pallas kernels: 0 us -> 10.8 us
  matrix products: 4.84 us -> 0 us
    psum x2 -> x0, waiting for transfers between devices: 210 us -> none  [spread(): return lax.psum(block, axis)]
    all_gather x1 -> x0, waiting for transfers between devices: 87.4 us -> none  [on_device(): everything = lax.all_gather(panel, 'row', axis=0, tiled=True)]
    ppermute x0 -> x22, starting transfers between devices: none -> 37.6 us  [move(): return lax.ppermute(block, AXES, pairs)]
    another operation x5 -> x0, other arithmetic: 22.9 us -> none  [the longest x3 12.5 us: on_device(): lower = jnp.linalg.cholesky(pivot)]
    ppermute x0 -> x22, waiting for transfers between devices: none -> 10.8 us  [move(): return lax.ppermute(block, AXES, pairs)]
    pallas_call x0 -> x4, Pallas kernels: none -> 10.8 us  [the longest x3 6.34 us: update(): pl.pallas_call(kernel, out_shape=jax.ShapeDtypeStruct(matrix.shape, jnp.f...]
    concatenate x1 -> x2, other arithmetic: 4.63 us -> 0.03 us  [the longest x1 0.02 us: on_device(): jnp.concatenate([move(near_b[:2 * NB], lambda X, Y, Z, C: (X ^ 1, Y, Z, C...]
    slice x1 -> x3, local copies, waits for them, and re-layouts: 4.33 us -> 0.03 us  [the longest x1 0.01 us: on_device(): panel[NB:]]
  transfers between devices with their start and end apart: 3 -> 22, of which waited for: 3 -> 8; matrix products, arithmetic and copies ran while one was open for 1% -> 2% of each run, Pallas kernels for 0% -> 14%
where the time goes in v2:
time: 62.2 us; the launch traced here: 61.9 us
  starting transfers between devices  37.6 us (60%)
  waiting for transfers between devices  10.8 us (17%)
  Pallas kernels  10.8 us (17%)
  other arithmetic  2.12 us (3%)
    ppermute x22, starting transfers between devices, move(): return lax.ppermute(block, AXES, pairs)  37.6 us
    ppermute x22, waiting for transfers between devices, move(): return lax.ppermute(block, AXES, pairs)  10.8 us
    pallas_call x3, Pallas kernels, update(): pl.pallas_call(kernel, out_shape=jax.ShapeDtypeStruct(matrix.shape, jnp.f...  6.34 us
    pallas_call x1, Pallas kernels, on_device(): pl.pallas_call(factor_kernel, out_shape=(tile, tile), in_specs=[vmem(), v...  4.47 us
  transfers between devices with their start and end apart: 22, of which 8 were waited for; matrix products, arithmetic and copies ran while one was open for 2% of the time, Pallas kernels for 14%

profile of v2, /device:TPU:1, one launch (start us, length us, event | category | flops | bytes accessed | tf_op | source)
XLA Modules:
  0.0 61.9 jit_solution(16757588858954333901)
XLA Ops:
  0.0 1.0 %slice_select_fusion.refs_1_ = f32[256,128]{1,0:T(8,128)S(1)} fusion(f32[256,4096]{1,0:T(8,128)} %refs_0_.5, pred[256]{0:T(512)(128)(4,1)S(1)} %compare_or_fusion), kind=kLoop, calls=%fused_computation.2 | loop fusion | flops 32768 | bytes 262400 | tf_op jit(solution)/shard_map/jit(_where)/select_n | solution.py:240
  1.0 4.6 %collective-permute-start.1 = (f32[128,128]{1,0:T(8,128)S(1)}, f32[128,128]{1,0:T(8,128)S(1)}, u32[]{:S(2)}, u32[]{:S(2)}) collective-permute-start(f32[128,128]{1,0:T(8,128)S(1)} %get-tuple-element.27), channel_id=1, source_target_pairs={{0,0},{4,1},{8,10},{12,11},{16,16},{20,17},{24,26},{28,27},{32,32}... | collective-permute-start | bytes 196616 | tf_op jit(solution)/shard_map/ppermute | solution.py:29
  5.6 1.9 %collective-permute-start = (f32[128,128]{1,0:T(8,128)S(1)}, f32[128,128]{1,0:T(8,128)S(1)}, u32[]{:S(2)}, u32[]{:S(2)}) collective-permute-start(f32[128,128]{1,0:T(8,128)S(1)} %get-tuple-element.21), channel_id=1, source_target_pairs={{0,4},{4,5},{8,14},{12,15},{16,20},{20,21},{24,30},{28,31},{32,36}... | collective-permute-start | bytes 196616 | tf_op jit(solution)/shard_map/ppermute | solution.py:29
  7.7 1.2 %collective-permute-done = f32[128,128]{1,0:T(8,128)S(1)} collective-permute-done((f32[128,128]{1,0:T(8,128)S(1)}, f32[128,128]{1,0:T(8,128)S(1)}, u32[]{:S(2)}, u32[]{:S(2)}) %collective-permute-start) | collective-permute-done | bytes 65568 | tf_op jit(solution)/shard_map/ppermute | solution.py:29
  8.9 3.3 %collective-permute-done.2.refs_2_ = f32[256,128]{1,0:T(8,128)S(1)} collective-permute-done((f32[256,128]{1,0:T(8,128)S(1)}, f32[256,128]{1,0:T(8,128)S(1)}, u32[]{:S(2)}, u32[]{:S(2)}) %collective-permute-start.2) | collective-permute-done | bytes 131104 | tf_op jit(solution)/shard_map/ppermute | solution.py:29
  12.2 8.2 %collective-permute-start.13 = (f32[128,128]{1,0:T(8,128)S(1)}, f32[128,128]{1,0:T(8,128)S(1)}, u32[]{:S(2)}, u32[]{:S(2)}) collective-permute-start(f32[128,128]{1,0:T(8,128)S(1)} %get-tuple-element.21), channel_id=1, source_target_pairs={{4,60},{5,61}} | collective-permute-start | bytes 196616 | tf_op jit(solution)/shard_map/ppermute | solution.py:29
  20.5 1.3 %collective-permute-start.3 = (f32[128,128]{1,0:T(8,128)S(1)}, f32[128,128]{1,0:T(8,128)S(1)}, u32[]{:S(2)}, u32[]{:S(2)}) collective-permute-start(f32[128,128]{1,0:T(8,128)S(1)} %broadcast_select_fusion.8), channel_id=1, source_target_pairs={{0,56},{1,57},{4,60},{5,61},{10,50},{11,51},{14,54},{15,55},{16,40... | collective-permute-start | bytes 196616 | tf_op jit(solution)/shard_map/ppermute | solution.py:29
  21.8 3.4 %collective-permute-start.14 = (f32[128,128]{1,0:T(8,128)S(1)}, f32[128,128]{1,0:T(8,128)S(1)}, u32[]{:S(2)}, u32[]{:S(2)}) collective-permute-start(f32[128,128]{1,0:T(8,128)S(1)} %broadcast_select_fusion.1), channel_id=1, source_target_pairs={{4,20},{5,21},{60,44},{61,45}} | collective-permute-start | bytes 196616 | tf_op jit(solution)/shard_map/ppermute | solution.py:29
  25.2 1.0 %broadcast_select_fusion = f32[256,128]{1,0:T(8,128)S(1)} fusion(f32[256,128]{1,0:T(8,128)S(1)} %collective-permute-done.2.refs_2_, pred[]{:T(512)S(6)} %eq.48, f32[256,4096]{1,0:T(8,128)} %refs_0_.5, pred[256]{0:T(512)(128)(4,1)S(1)} %compare_or_fusion), kind=kLoop, calls=%fused_computation.3 | loop fusion | flops 65536 | bytes 393473 | tf_op jit(solution)/shard_map/jit(_where)/select_n | solution.py:251
  26.5 1.3 %collective-permute-start.15 = (f32[128,128]{1,0:T(8,128)S(1)}, f32[128,128]{1,0:T(8,128)S(1)}, u32[]{:S(2)}, u32[]{:S(2)}) collective-permute-start(f32[128,128]{1,0:T(8,128)S(1)} %broadcast_select_fusion.2), channel_id=1, source_target_pairs={{4,12},{5,13},{20,28},{21,29},{44,36},{45,37},{60,52},{61,53}} | collective-permute-start | bytes 196616 | tf_op jit(solution)/shard_map/ppermute | solution.py:29
  27.9 2.8 %collective-permute-start.4 = (f32[128,128]{1,0:T(8,128)S(1)}, f32[128,128]{1,0:T(8,128)S(1)}, u32[]{:S(2)}, u32[]{:S(2)}) collective-permute-start(f32[128,128]{1,0:T(8,128)S(1)} %broadcast_select_fusion.7), channel_id=1, source_target_pairs={{0,16},{1,17},{2,18},{3,19},{4,20},{5,21},{6,22},{7,23},{8,24},{9,... | collective-permute-start | bytes 196616 | tf_op jit(solution)/shard_map/ppermute | solution.py:29
  30.6 1.3 %collective-permute-start.16 = (f32[128,128]{1,0:T(8,128)S(1)}, f32[128,128]{1,0:T(8,128)S(1)}, u32[]{:S(2)}, u32[]{:S(2)}) collective-permute-start(f32[128,128]{1,0:T(8,128)S(1)} %broadcast_select_fusion.3), channel_id=1, source_target_pairs={{4,132},{5,133},{12,140},{13,141},{20,148},{21,149},{28,156},{29,1... | collective-permute-start | bytes 196616 | tf_op jit(solution)/shard_map/ppermute | solution.py:29
  33.3 1.3 %collective-permute-start.17 = (f32[128,128]{1,0:T(8,128)S(1)}, f32[128,128]{1,0:T(8,128)S(1)}, u32[]{:S(2)}, u32[]{:S(2)}) collective-permute-start(f32[128,128]{1,0:T(8,128)S(1)} %broadcast_select_fusion.4), channel_id=1, source_target_pairs={{4,68},{5,69},{12,76},{13,77},{20,84},{21,85},{28,92},{29,93},{36,... | collective-permute-start | bytes 196616 | tf_op jit(solution)/shard_map/ppermute | solution.py:29
  34.6 1.3 %collective-permute-done.17 = f32[128,128]{1,0:T(8,128)S(1)} collective-permute-done((f32[128,128]{1,0:T(8,128)S(1)}, f32[128,128]{1,0:T(8,128)S(1)}, u32[]{:S(2)}, u32[]{:S(2)}) %collective-permute-start.17) | collective-permute-done | bytes 65568 | tf_op jit(solution)/shard_map/ppermute | solution.py:29
  35.9 1.3 %collective-permute-start.18 = (f32[128,128]{1,0:T(8,128)S(1)}, f32[128,128]{1,0:T(8,128)S(1)}, u32[]{:S(2)}, u32[]{:S(2)}) collective-permute-start(f32[128,128]{1,0:T(8,128)S(1)} %broadcast_select_fusion.5), channel_id=1, source_target_pairs={{4,0},{5,1},{12,8},{13,9},{20,16},{21,17},{28,24},{29,25},{36,32},... | collective-permute-start | bytes 196616 | tf_op jit(solution)/shard_map/ppermute | solution.py:29
  37.2 4.0 %collective-permute-start.10 = (f32[512,128]{1,0:T(8,128)S(1)}, f32[512,128]{1,0:T(8,128)S(1)}, u32[]{:S(2)}, u32[]{:S(2)}) collective-permute-start(f32[512,128]{1,0:T(8,128)S(1)} %constant_dynamic-update-slice_fusion.refs_4_), channel_id=1, source_target_pairs={{0,192},{1,193},{2,194},{3,195},{4,196},{5,197},{6,198},{7,199},{8... | collective-permute-start | bytes 786440 | tf_op jit(solution)/shard_map/ppermute | solution.py:29
  41.2 2.4 %collective-permute-start.19 = (f32[128,128]{1,0:T(8,128)S(1)}, f32[128,128]{1,0:T(8,128)S(1)}, u32[]{:S(2)}, u32[]{:S(2)}) collective-permute-start(f32[128,128]{1,0:T(8,128)S(1)} %broadcast_select_fusion.6.a_ref), channel_id=1, source_target_pairs={{0,1},{4,5},{8,9},{12,13},{16,17},{20,21},{24,25},{28,29},{32,33},... | collective-permute-start | bytes 196616 | tf_op jit(solution)/shard_map/ppermute | solution.py:29
  43.8 3.6 %collective-permute-done.10.refs_6_.refs_10_ = f32[512,128]{1,0:T(8,128)S(1)} collective-permute-done((f32[512,128]{1,0:T(8,128)S(1)}, f32[512,128]{1,0:T(8,128)S(1)}, u32[]{:S(2)}, u32[]{:S(2)}) %collective-permute-start.10) | collective-permute-done | bytes 262176 | tf_op jit(solution)/shard_map/ppermute | solution.py:29
  47.9 1.4 %collective-permute-start.12 = (f32[256,128]{1,0:T(8,128)S(1)}, f32[256,128]{1,0:T(8,128)S(1)}, u32[]{:S(2)}, u32[]{:S(2)}) collective-permute-start(f32[256,128]{1,0:T(8,128)S(1)} %slice.24), channel_id=1, source_target_pairs={{0,192},{1,193},{2,194},{3,195},{4,196},{5,197},{6,198},{7,199},{8... | collective-permute-start | bytes 393224 | tf_op jit(solution)/shard_map/ppermute | solution.py:29
  49.3 4.5 %shard_map.17 = (f32[128,128]{1,0:T(8,128)S(1)}, f32[128,128]{1,0:T(8,128)S(1)}) custom-call(f32[128,128]{1,0:T(8,128)S(1)} %broadcast_select_fusion.6.a_ref, f32[128,128]{1,0:T(8,128)S(1)} %collective-permute-done.19.p_ref), custom_call_target="tpu_custom_call" | custom-call | flops 6000000000 | bytes 196608 | tf_op jit(solution)/shard_map/pallas_call | solution.py:295
  53.8 0.8 %collective-permute-start.21 = (f32[512,128]{1,0:T(8,128)S(1)}, f32[512,128]{1,0:T(8,128)S(1)}, u32[]{:S(2)}, u32[]{:S(2)}) collective-permute-start(f32[512,128]{1,0:T(8,128)S(1)} %collective-permute-done.10.refs_6_.refs_10_), channel_id=1, source_target_pairs={{0,4},{1,5},{2,6},{3,7},{4,0},{5,1},{6,2},{7,3},{8,12},{9,13},{10,... | collective-permute-start | bytes 786440 | tf_op jit(solution)/shard_map/ppermute | solution.py:29
  55.4 1.7 %shard_map.18.refs_8_ = f32[256,4096]{1,0:T(8,128)} custom-call(f32[256,4096]{1,0:T(8,128)S(1)} %copy-done, f32[256,128]{1,0:T(8,128)S(1)} %slice_select_fusion.refs_1_, f32[256,128]{1,0:T(8,128)S(1)} %collective-permute-done.2.refs_2_, f32[256,128]{1,0:T(8,128)S(1)} %collective-permute-done.5.refs_3_, ...), custom_call_target="tpu_custom_call" | custom-call | flops 268435456 | bytes 2097152 | tf_op jit(solution)/shard_map/pallas_call | solution.py:219
  57.1 2.6 %shard_map.19.refs_14_ = f32[256,4096]{1,0:T(8,128)} custom-call(f32[256,4096]{1,0:T(8,128)S(1)} %copy-done, f32[256,128]{1,0:T(8,128)S(1)} %slice_select_fusion.refs_1_, f32[256,128]{1,0:T(8,128)S(1)} %collective-permute-done.2.refs_2_, f32[256,128]{1,0:T(8,128)S(1)} %collective-permute-done.5.refs_3_, ...), custom_call_target="tpu_custom_call", output_to_operand_aliasing={{}: (8, {})} | custom-call | flops 536870912 | bytes 4194304 | tf_op jit(solution)/shard_map/pallas_call | solution.py:219
  59.8 2.0 %shard_map.20 = f32[256,4096]{1,0:T(8,128)} custom-call(f32[256,4096]{1,0:T(8,128)S(1)} %copy-done, f32[256,128]{1,0:T(8,128)S(1)} %slice_select_fusion.refs_1_, f32[256,128]{1,0:T(8,128)S(1)} %collective-permute-done.2.refs_2_, f32[256,128]{1,0:T(8,128)S(1)} %collective-permute-done.5.refs_3_, ...), custom_call_target="tpu_custom_call", output_to_operand_aliasing={{}: (14, {})} | custom-call | flops 268435456 | bytes 2097152 | tf_op jit(solution)/shard_map/pallas_call | solution.py:219
  (44 shorter events, 3.3 us)
Async XLA Ops:
  1.0 6.6 %collective-permute-start.1 = (f32[128,128]{1,0:T(8,128)S(1)}, f32[128,128]{1,0:T(8,128)S(1)}, u32[]{:S(2)}, u32[]{:S(2)}) collective-permute-start(f32[128,128]{1,0:T(8,128)S(1)} %get-tuple-element.27), channel_id=1, source_target_pairs={{0,0},{4,1},{8,10},{12,11},{16,16},{20,17},{24,26},{28,27},{32,32}... | collective-permute-start | bytes 196616 | tf_op jit(solution)/shard_map/ppermute | solution.py:29
  5.6 3.2 %collective-permute-start = (f32[128,128]{1,0:T(8,128)S(1)}, f32[128,128]{1,0:T(8,128)S(1)}, u32[]{:S(2)}, u32[]{:S(2)}) collective-permute-start(f32[128,128]{1,0:T(8,128)S(1)} %get-tuple-element.21), channel_id=1, source_target_pairs={{0,4},{4,5},{8,14},{12,15},{16,20},{20,21},{24,30},{28,31},{32,36}... | collective-permute-start | bytes 196616 | tf_op jit(solution)/shard_map/ppermute | solution.py:29
  7.6 4.7 %collective-permute-start.2 = (f32[256,128]{1,0:T(8,128)S(1)}, f32[256,128]{1,0:T(8,128)S(1)}, u32[]{:S(2)}, u32[]{:S(2)}) collective-permute-start(f32[256,128]{1,0:T(8,128)S(1)} %slice_select_fusion.refs_1_), channel_id=1, source_target_pairs={{0,1},{1,0},{2,3},{3,2},{4,5},{5,4},{6,7},{7,6},{8,9},{9,8},{10,11... | collective-permute-start | bytes 393224 | tf_op jit(solution)/shard_map/ppermute | solution.py:29
  12.2 9.6 %collective-permute-start.13 = (f32[128,128]{1,0:T(8,128)S(1)}, f32[128,128]{1,0:T(8,128)S(1)}, u32[]{:S(2)}, u32[]{:S(2)}) collective-permute-start(f32[128,128]{1,0:T(8,128)S(1)} %get-tuple-element.21), channel_id=1, source_target_pairs={{4,60},{5,61}} | collective-permute-start | bytes 196616 | tf_op jit(solution)/shard_map/ppermute | solution.py:29
  20.5 7.3 %collective-permute-start.3 = (f32[128,128]{1,0:T(8,128)S(1)}, f32[128,128]{1,0:T(8,128)S(1)}, u32[]{:S(2)}, u32[]{:S(2)}) collective-permute-start(f32[128,128]{1,0:T(8,128)S(1)} %broadcast_select_fusion.8), channel_id=1, source_target_pairs={{0,56},{1,57},{4,60},{5,61},{10,50},{11,51},{14,54},{15,55},{16,40... | collective-permute-start | bytes 196616 | tf_op jit(solution)/shard_map/ppermute | solution.py:29
  21.8 4.7 %collective-permute-start.14 = (f32[128,128]{1,0:T(8,128)S(1)}, f32[128,128]{1,0:T(8,128)S(1)}, u32[]{:S(2)}, u32[]{:S(2)}) collective-permute-start(f32[128,128]{1,0:T(8,128)S(1)} %broadcast_select_fusion.1), channel_id=1, source_target_pairs={{4,20},{5,21},{60,44},{61,45}} | collective-permute-start | bytes 196616 | tf_op jit(solution)/shard_map/ppermute | solution.py:29
  26.2 6.1 %collective-permute-start.5 = (f32[256,128]{1,0:T(8,128)S(1)}, f32[256,128]{1,0:T(8,128)S(1)}, u32[]{:S(2)}, u32[]{:S(2)}) collective-permute-start(f32[256,128]{1,0:T(8,128)S(1)} %broadcast_select_fusion), channel_id=1, source_target_pairs={{0,3},{1,2},{2,1},{3,0},{4,7},{5,6},{6,5},{7,4},{8,11},{9,10},{10,... | collective-permute-start | bytes 393224 | tf_op jit(solution)/shard_map/ppermute | solution.py:29
  26.5 4.1 %collective-permute-start.15 = (f32[128,128]{1,0:T(8,128)S(1)}, f32[128,128]{1,0:T(8,128)S(1)}, u32[]{:S(2)}, u32[]{:S(2)}) collective-permute-start(f32[128,128]{1,0:T(8,128)S(1)} %broadcast_select_fusion.2), channel_id=1, source_target_pairs={{4,12},{5,13},{20,28},{21,29},{44,36},{45,37},{60,52},{61,53}} | collective-permute-start | bytes 196616 | tf_op jit(solution)/shard_map/ppermute | solution.py:29
  27.9 4.4 %collective-permute-start.4 = (f32[128,128]{1,0:T(8,128)S(1)}, f32[128,128]{1,0:T(8,128)S(1)}, u32[]{:S(2)}, u32[]{:S(2)}) collective-permute-start(f32[128,128]{1,0:T(8,128)S(1)} %broadcast_select_fusion.7), channel_id=1, source_target_pairs={{0,16},{1,17},{2,18},{3,19},{4,20},{5,21},{6,22},{7,23},{8,24},{9,... | collective-permute-start | bytes 196616 | tf_op jit(solution)/shard_map/ppermute | solution.py:29
  30.6 2.6 %collective-permute-start.16 = (f32[128,128]{1,0:T(8,128)S(1)}, f32[128,128]{1,0:T(8,128)S(1)}, u32[]{:S(2)}, u32[]{:S(2)}) collective-permute-start(f32[128,128]{1,0:T(8,128)S(1)} %broadcast_select_fusion.3), channel_id=1, source_target_pairs={{4,132},{5,133},{12,140},{13,141},{20,148},{21,149},{28,156},{29,1... | collective-permute-start | bytes 196616 | tf_op jit(solution)/shard_map/ppermute | solution.py:29
  32.3 4.9 %collective-permute-start.6 = (f32[256,128]{1,0:T(8,128)S(1)}, f32[256,128]{1,0:T(8,128)S(1)}, u32[]{:S(2)}, u32[]{:S(2)}) collective-permute-start(f32[256,128]{1,0:T(8,128)S(1)} %pad_maximum_fusion.1), channel_id=1, source_target_pairs={{0,8},{1,9},{2,10},{3,11},{4,12},{5,13},{6,14},{7,15},{8,0},{9,1},... | collective-permute-start | bytes 393224 | tf_op jit(solution)/shard_map/ppermute | solution.py:29
  33.3 2.6 %collective-permute-start.17 = (f32[128,128]{1,0:T(8,128)S(1)}, f32[128,128]{1,0:T(8,128)S(1)}, u32[]{:S(2)}, u32[]{:S(2)}) collective-permute-start(f32[128,128]{1,0:T(8,128)S(1)} %broadcast_select_fusion.4), channel_id=1, source_target_pairs={{4,68},{5,69},{12,76},{13,77},{20,84},{21,85},{28,92},{29,93},{36,... | collective-permute-start | bytes 196616 | tf_op jit(solution)/shard_map/ppermute | solution.py:29
  35.9 5.3 %collective-permute-start.18 = (f32[128,128]{1,0:T(8,128)S(1)}, f32[128,128]{1,0:T(8,128)S(1)}, u32[]{:S(2)}, u32[]{:S(2)}) collective-permute-start(f32[128,128]{1,0:T(8,128)S(1)} %broadcast_select_fusion.5), channel_id=1, source_target_pairs={{4,0},{5,1},{12,8},{13,9},{20,16},{21,17},{28,24},{29,25},{36,32},... | collective-permute-start | bytes 196616 | tf_op jit(solution)/shard_map/ppermute | solution.py:29
  37.2 10.1 %collective-permute-start.10 = (f32[512,128]{1,0:T(8,128)S(1)}, f32[512,128]{1,0:T(8,128)S(1)}, u32[]{:S(2)}, u32[]{:S(2)}) collective-permute-start(f32[512,128]{1,0:T(8,128)S(1)} %constant_dynamic-update-slice_fusion.refs_4_), channel_id=1, source_target_pairs={{0,192},{1,193},{2,194},{3,195},{4,196},{5,197},{6,198},{7,199},{8... | collective-permute-start | bytes 786440 | tf_op jit(solution)/shard_map/ppermute | solution.py:29
  41.2 6.7 %collective-permute-start.8 = (f32[512,128]{1,0:T(8,128)S(1)}, f32[512,128]{1,0:T(8,128)S(1)}, u32[]{:S(2)}, u32[]{:S(2)}) collective-permute-start(f32[512,128]{1,0:T(8,128)S(1)} %constant_dynamic-update-slice_fusion.refs_4_), channel_id=1, source_target_pairs={{0,64},{1,65},{2,66},{3,67},{4,68},{5,69},{6,70},{7,71},{8,72},{9,... | collective-permute-start | bytes 786440 | tf_op jit(solution)/shard_map/ppermute | solution.py:29
  41.2 8.1 %collective-permute-start.19 = (f32[128,128]{1,0:T(8,128)S(1)}, f32[128,128]{1,0:T(8,128)S(1)}, u32[]{:S(2)}, u32[]{:S(2)}) collective-permute-start(f32[128,128]{1,0:T(8,128)S(1)} %broadcast_select_fusion.6.a_ref), channel_id=1, source_target_pairs={{0,1},{4,5},{8,9},{12,13},{16,17},{20,21},{24,25},{28,29},{32,33},... | collective-permute-start | bytes 196616 | tf_op jit(solution)/shard_map/ppermute | solution.py:29
  43.7 11.7 %collective-permute-start.7 = (f32[512,128]{1,0:T(8,128)S(1)}, f32[512,128]{1,0:T(8,128)S(1)}, u32[]{:S(2)}, u32[]{:S(2)}) collective-permute-start(f32[512,128]{1,0:T(8,128)S(1)} %constant_dynamic-update-slice_fusion.refs_4_), channel_id=1, source_target_pairs={{0,4},{1,5},{2,6},{3,7},{4,0},{5,1},{6,2},{7,3},{8,12},{9,13},{10,... | collective-permute-start | bytes 786440 | tf_op jit(solution)/shard_map/ppermute | solution.py:29
  47.4 7.2 %collective-permute-start.11 = (f32[256,128]{1,0:T(8,128)S(1)}, f32[256,128]{1,0:T(8,128)S(1)}, u32[]{:S(2)}, u32[]{:S(2)}) collective-permute-start(f32[256,128]{1,0:T(8,128)S(1)} %slice.23), channel_id=1, source_target_pairs={{0,64},{1,65},{2,66},{3,67},{4,68},{5,69},{6,70},{7,71},{8,72},{9,... | collective-permute-start | bytes 393224 | tf_op jit(solution)/shard_map/ppermute | solution.py:29
  47.9 7.5 %copy-start = (f32[256,4096]{1,0:T(8,128)S(1)}, f32[256,4096]{1,0:T(8,128)}, u32[]{:S(2)}) copy-start(f32[256,4096]{1,0:T(8,128)} %refs_0_.5) | copy-start | bytes 12582916
  47.9 6.7 %collective-permute-start.12 = (f32[256,128]{1,0:T(8,128)S(1)}, f32[256,128]{1,0:T(8,128)S(1)}, u32[]{:S(2)}, u32[]{:S(2)}) collective-permute-start(f32[256,128]{1,0:T(8,128)S(1)} %slice.24), channel_id=1, source_target_pairs={{0,192},{1,193},{2,194},{3,195},{4,196},{5,197},{6,198},{7,199},{8... | collective-permute-start | bytes 393224 | tf_op jit(solution)/shard_map/ppermute | solution.py:29
  53.8 3.4 %collective-permute-start.21 = (f32[512,128]{1,0:T(8,128)S(1)}, f32[512,128]{1,0:T(8,128)S(1)}, u32[]{:S(2)}, u32[]{:S(2)}) collective-permute-start(f32[512,128]{1,0:T(8,128)S(1)} %collective-permute-done.10.refs_6_.refs_10_), channel_id=1, source_target_pairs={{0,4},{1,5},{2,6},{3,7},{4,0},{5,1},{6,2},{7,3},{8,12},{9,13},{10,... | collective-permute-start | bytes 786440 | tf_op jit(solution)/shard_map/ppermute | solution.py:29
  54.5 2.6 %collective-permute-start.9 = (f32[512,128]{1,0:T(8,128)S(1)}, f32[512,128]{1,0:T(8,128)S(1)}, u32[]{:S(2)}, u32[]{:S(2)}) collective-permute-start(f32[512,128]{1,0:T(8,128)S(1)} %collective-permute-done.8.refs_4_.refs_6_), channel_id=1, source_target_pairs={{0,4},{1,5},{2,6},{3,7},{4,0},{5,1},{6,2},{7,3},{8,12},{9,13},{10,... | collective-permute-start | bytes 786440 | tf_op jit(solution)/shard_map/ppermute | solution.py:29
  54.6 5.1 %collective-permute-start.20 = (f32[512,128]{1,0:T(8,128)S(1)}, f32[512,128]{1,0:T(8,128)S(1)}, u32[]{:S(2)}, u32[]{:S(2)}) collective-permute-start(f32[512,128]{1,0:T(8,128)S(1)} %pad_maximum_fusion.refs_8_), channel_id=1, source_target_pairs={{0,4},{1,5},{2,6},{3,7},{4,0},{5,1},{6,2},{7,3},{8,12},{9,13},{10,... | collective-permute-start | bytes 786440 | tf_op jit(solution)/shard_map/ppermute | solution.py:29

commit v3 on v2

--- a/solution.py
+++ b/solution.py
@@ -6,6 +6,7 @@
 from jax.sharding import PartitionSpec as P
 
 NB = 128
+HALF = NB // 2
 NX, NY, NZ, NC = 4, 4, 8, 2
 AXES = ("row", "col")
 HIGH = lax.Precision.HIGHEST
@@ -43,7 +44,26 @@
     return both + lax.dot_general(left_hi, lo, TRANS, preferred_element_type=jnp.float32)
 
 
+def place():
+    row = lax.axis_index("row")
+    return row // (NZ * NC), row // NC % NZ, row % NC, lax.axis_index("col"), row
+
+
 def factor_kernel(a_ref, p_ref, low_ref, inv_ref, u_ref):
+    x, z, core, y, row = place()
+    here = (row == 1) & (y == 1)
+
+    @pl.when(here)
+    def _():
+        factor(a_ref, p_ref, low_ref, inv_ref, u_ref)
+
+    @pl.when(jnp.logical_not(here))
+    def _():
+        low_ref[...] = jnp.zeros((NB, NB), jnp.float32)
+        inv_ref[...] = jnp.zeros((NB, NB), jnp.float32)
+
+
+def factor(a_ref, p_ref, low_ref, inv_ref, u_ref):
     p = p_ref[...]
     u_ref[...] = a_ref[...] - lax.dot_general(
         p, p, TRANS, precision=HIGH, preferred_element_type=jnp.float32
@@ -88,9 +108,9 @@
     low_ref[...] = jnp.concatenate(upper, axis=0).T
 
 
-def place():
-    row = lax.axis_index("row")
-    return row // (NZ * NC), row // NC % NZ, row % NC, lax.axis_index("col"), row
+def forward_kernel(panel_ref, rows_ref, out_ref):
+    x, z, core, y, row = place()
+    out_ref[...] = jnp.where(y == 1, rows_ref[...], panel_ref[...])
 
 
 def panels(y, p_ref):
@@ -154,7 +174,7 @@
     outs = []
     for i, (e, s) in enumerate(groups):
         ref = pieces[2 * e + s] if last else pieces[i]
-        prod = times_transposed(hi, both, ref[...])
+        prod = times_transposed(hi, both, ref[: 4 * NB, :])
         ins[i].wait()
         for d in range(4):
             cols = pl.ds(pl.multiple_of(slots[d] * NB, NB), NB)
@@ -245,54 +265,7 @@
     got_b = move(panel[NB:], lambda X, Y, Z, C: (X, plane(X, Y, Z, C), Z, 0), source)
     piece = jnp.where(core == 1, got_a, got_b)
 
-    rows_a = move(panel, lambda X, Y, Z, C: (X, Y ^ 1, Z, C))
-    piece, rows_a = lax.optimization_barrier((piece, rows_a))
-    rows_b = move(
-        jnp.where(y == 1, rows_a, panel), lambda X, Y, Z, C: (X, Y ^ 3, Z, C)
-    )
-
-    tile_of = lambda X, Y, Z, C: Y < 2 and (X, Z, C) == (0, 0, 1)
-    seed, piece = lax.optimization_barrier((panel[:NB], piece))
-    got = move(seed, lambda X, Y, Z, C: (X, Y, 7, C), tile_of)
-    seed = jnp.where(z == 7, got, seed)
-    got = move(
-        seed,
-        lambda X, Y, Z, C: (X, Y, Z ^ 2, C),
-        lambda X, Y, Z, C: Y < 2 and X == 0 and C == 1 and Z in (0, 7),
-    )
-    seed = jnp.where((z == 2) | (z == 5), got, seed)
-    got = move(
-        seed,
-        lambda X, Y, Z, C: (X, Y, Z ^ 1, C),
-        lambda X, Y, Z, C: Y < 2 and X == 0 and C == 1 and Z in (0, 2, 5, 7),
-    )
-    seed = jnp.where((z == 1) | (z == 3) | (z == 4) | (z == 6), got, seed)
-    got = move(
-        seed,
-        lambda X, Y, Z, C: (2, Y, Z, C),
-        lambda X, Y, Z, C: Y < 2 and X == 0 and C == 1,
-    )
-    seed = jnp.where(x == 2, got, seed)
-    got = move(
-        seed,
-        lambda X, Y, Z, C: (X + 1, Y, Z, C),
-        lambda X, Y, Z, C: Y < 2 and X in (0, 2) and C == 1,
-    )
-    seed = jnp.where((x == 1) | (x == 3), got, seed)
-    got = move(seed, lambda X, Y, Z, C: (X, Y, Z, 0), lambda X, Y, Z, C: Y < 2 and C == 1)
-    seed = jnp.where(core == 0, got, seed)
-    pivot_rows = move(seed, lambda X, Y, Z, C: (X, 1, Z, C), lambda X, Y, Z, C: Y == 0)
-
-    holds = lambda X, Y, Z, C: Z % 2 == Y // 2
-    mirrored = move(piece, lambda X, Y, Z, C: (X, Y, 7 - Z, C), holds)
-    piece = jnp.where(z % 2 == y // 2, piece, mirrored)
-
-    two = jnp.concatenate([piece, move(piece, lambda X, Y, Z, C: (X, Y, Z ^ 2, C))])
-    two, rows_b = lax.optimization_barrier((two, rows_b))
-    cands = [panel, rows_a, rows_b]
-    four = jnp.concatenate([two, move(two, lambda X, Y, Z, C: (X, Y, Z ^ 1, C))])
-
-    factors = pl.pallas_call(
+    lower, inverse = pl.pallas_call(
         factor_kernel,
         out_shape=(tile, tile),
         in_specs=[vmem(), vmem()],
@@ -300,28 +273,67 @@
         scratch_shapes=[pltpu.VMEM((NB, NB), jnp.float32)],
         compiler_params=pltpu.CompilerParams(vmem_limit_bytes=8 * MIB),
         cost_estimate=pl.CostEstimate(
-            flops=6 * 10**9, bytes_accessed=3 * NB * NB * 4, transcendentals=0
+            flops=10**8, bytes_accessed=3 * NB * NB * 4, transcendentals=0
         ),
-    )(seed, pivot_rows)
-
+    )(panel[:NB], piece)
     other = lambda X, Y, Z, C: (X, Y, Z, 1 - C)
-    near_a = move(four, lambda X, Y, Z, C: (X ^ 1, Y, Z, C))
-    near_b = move(four, lambda X, Y, Z, C: (X ^ 3, Y, Z, C))
+    seed = jnp.where(core == 1, inverse[HALF:], move(inverse[:HALF], other))
+    own, piece = lax.optimization_barrier((panel, piece))
+
+    holds = lambda X, Y, Z, C: Z % 2 == Y // 2
+    mirrored = move(jnp.concatenate([piece, seed]), lambda X, Y, Z, C: (X, Y, 7 - Z, C), holds)
+
+    rows_a = move(own, lambda X, Y, Z, C: (X, Y ^ 1, Z, C))
+    mirrored, rows_a = lax.optimization_barrier((mirrored, rows_a))
+    holder = z % 2 == y // 2
+    piece = jnp.where(holder, piece, mirrored[:NB])
+    seed = jnp.where(z == 7, mirrored[NB:], seed)
+
+    got = move(jnp.concatenate([piece, seed]), lambda X, Y, Z, C: (X, Y, Z ^ 2, C))
+    two = jnp.concatenate([piece, got[:NB]])
+    seed = jnp.where((z == 2) | (z == 5), got[NB:], seed)
+    got = move(jnp.concatenate([two, seed]), lambda X, Y, Z, C: (X, Y, Z ^ 1, C))
+    four = jnp.concatenate([two, got[: 2 * NB]])
+    seed = jnp.where((z == 0) | (z == 2) | (z == 5) | (z == 7), seed, got[2 * NB :])
+
+    full = jnp.concatenate([four, seed])
+    near_a = move(full, lambda X, Y, Z, C: (X ^ 1, Y, Z, C))
+    near_b = move(full, lambda X, Y, Z, C: (X ^ 3, Y, Z, C))
     four_o = move(four, other)
-    far = jnp.concatenate(
-        [
-            move(near_b[: 2 * NB], lambda X, Y, Z, C: (X ^ 1, Y, Z, C)),
-            move(near_a[2 * NB :], lambda X, Y, Z, C: (X ^ 3, Y, Z, C)),
-        ]
-    )
-    near_a_o, near_b_o = move(near_a, other), move(near_b, other)
-    far, factors = lax.optimization_barrier((far, factors))
+    forward = pl.pallas_call(
+        forward_kernel,
+        out_shape=jax.ShapeDtypeStruct(panel.shape, jnp.float32),
+        in_specs=[vmem(), vmem()],
+        out_specs=vmem(),
+        compiler_params=pltpu.CompilerParams(vmem_limit_bytes=8 * MIB),
+        cost_estimate=pl.CostEstimate(
+            flops=5 * 10**9, bytes_accessed=6 * NB * NB * 4, transcendentals=0
+        ),
+    )(panel, rows_a)
+    rows_b = move(forward, lambda X, Y, Z, C: (X, Y ^ 3, Z, C))
+    near_a, near_b, rows_b = lax.optimization_barrier((near_a, near_b, rows_b))
+    cands = [panel, rows_a, rows_b]
+    far_a = move(
+        jnp.concatenate([near_b[: 2 * NB], near_b[4 * NB :]]),
+        lambda X, Y, Z, C: (X ^ 1, Y, Z, C),
+    )
+    far_b = move(near_a[2 * NB : 4 * NB], lambda X, Y, Z, C: (X ^ 3, Y, Z, C))
+    near_a_o, near_b_o = move(near_a[: 4 * NB], other), move(near_b[: 4 * NB], other)
+    near = [four, four_o, near_a, near_a_o, near_b, near_b_o]
+    out = update((0, 1, 3), matrix, cands, near)
+    far_a, far_b, out = lax.optimization_barrier((far_a, far_b, out))
+    seed = jnp.where(x == 1, near_a[4 * NB :], seed)
+    seed = jnp.where(x == 3, near_b[4 * NB :], seed)
+    seed = jnp.where(x == 2, far_a[2 * NB :], seed)
+    far = jnp.concatenate([far_a[: 2 * NB], far_b, seed])
     far_o = move(far, other)
-
-    out = update((0,), matrix, cands, [four, four_o])
-    out = update((1, 3), matrix, cands, [near_a, near_a_o, near_b, near_b_o], out)
+    inverse = jnp.where(
+        core == 1,
+        jnp.concatenate([far_o[4 * NB :], seed]),
+        jnp.concatenate([seed, far_o[4 * NB :]]),
+    )
     pieces = [four, four_o, near_a, near_a_o, far, far_o, near_b, near_b_o]
-    return update((2,), matrix, cands, pieces, out, factors)
+    return update((2,), matrix, cands, pieces, out, (lower, inverse))
 
 
 def solution(mesh):

time: 62.2 us -> 57.5 us (0.924)
  Pallas kernels: 10.8 us -> 5.46 us
  local copies, waits for them, and re-layouts: 0.06 us -> 2.29 us
  waiting for transfers between devices: 10.8 us -> 9.82 us
  other arithmetic: 2.12 us -> 1.18 us
    pallas_call x1, Pallas kernels: 4.47 us -> 0.03 us  [on_device(): pl.pallas_call(factor_kernel, out_shape=(tile, tile), in_specs=[vmem(), v...]
    unnamed x3 -> x2, local copies, waits for them, and re-layouts: 0.02 us -> 2.18 us
    select_n x8 -> x7, other arithmetic: 1.07 us -> 0.06 us  [the longest x1 0.01 us: on_device(): seed = jnp.where(x == 2, far_a[2 * NB:], seed)]
    ppermute x22 -> x16, waiting for transfers between devices: 10.8 us -> 9.82 us  [move(): return lax.ppermute(block, AXES, pairs)]
    pallas_call x3 -> x2, Pallas kernels: 6.34 us -> 5.41 us  [update(): pl.pallas_call(kernel, out_shape=jax.ShapeDtypeStruct(matrix.shape, jnp.f...]
    ppermute x22 -> x16, starting transfers between devices: 37.6 us -> 38.1 us  [move(): return lax.ppermute(block, AXES, pairs)]
  transfers between devices with their start and end apart: 22 -> 16, of which waited for: 8 -> 5; matrix products, arithmetic and copies ran while one was open for 2% -> 0% of each run, Pallas kernels for 14% -> 6%
where the time goes in v3:
time: 57.5 us; the launch traced here: 57.3 us
  starting transfers between devices  38.1 us (66%)
  waiting for transfers between devices  9.82 us (17%)
  Pallas kernels  5.46 us (9%)
  local copies, waits for them, and re-layouts  2.29 us (4%)
  other arithmetic  1.18 us (2%)
    ppermute x16, starting transfers between devices, move(): return lax.ppermute(block, AXES, pairs)  38.1 us
    ppermute x16, waiting for transfers between devices, move(): return lax.ppermute(block, AXES, pairs)  9.82 us
    pallas_call x2, Pallas kernels, update(): pl.pallas_call(kernel, out_shape=jax.ShapeDtypeStruct(matrix.shape, jnp.f...  5.41 us
    unnamed x2, local copies, waits for them, and re-layouts  2.18 us
  transfers between devices with their start and end apart: 16, of which 5 were waited for; matrix products, arithmetic and copies ran while one was open for 0% of the time, Pallas kernels for 6%

profile of v3, /device:TPU:1, one launch (start us, length us, event | category | flops | bytes accessed | tf_op | source)
XLA Modules:
  0.0 57.3 jit_solution(10561130914091034290)
XLA Ops:
  0.0 1.0 %slice_select_fusion.panel_ref.refs_1_ = f32[256,128]{1,0:T(8,128)S(1)} fusion(f32[256,4096]{1,0:T(8,128)} %refs_0_.3, pred[256]{0:T(512)(128)(4,1)S(1)} %compare_or_fusion), kind=kLoop, calls=%fused_computation.5 | loop fusion | flops 32768 | bytes 262400 | tf_op jit(solution)/shard_map/jit(_where)/select_n | solution.py:260
  1.0 4.6 %collective-permute-start.1 = (f32[128,128]{1,0:T(8,128)S(1)}, f32[128,128]{1,0:T(8,128)S(1)}, u32[]{:S(2)}, u32[]{:S(2)}) collective-permute-start(f32[128,128]{1,0:T(8,128)S(1)} %get-tuple-element.29), channel_id=1, source_target_pairs={{0,0},{4,1},{8,10},{12,11},{16,16},{20,17},{24,26},{28,27},{32,32}... | collective-permute-start | bytes 196616 | tf_op jit(solution)/shard_map/ppermute | solution.py:30
  5.6 1.9 %collective-permute-start = (f32[128,128]{1,0:T(8,128)S(1)}, f32[128,128]{1,0:T(8,128)S(1)}, u32[]{:S(2)}, u32[]{:S(2)}) collective-permute-start(f32[128,128]{1,0:T(8,128)S(1)} %get-tuple-element.30.a_ref), channel_id=1, source_target_pairs={{0,4},{4,5},{8,14},{12,15},{16,20},{20,21},{24,30},{28,31},{32,36}... | collective-permute-start | bytes 196616 | tf_op jit(solution)/shard_map/ppermute | solution.py:30
  7.6 1.3 %collective-permute-done = f32[128,128]{1,0:T(8,128)S(1)} collective-permute-done((f32[128,128]{1,0:T(8,128)S(1)}, f32[128,128]{1,0:T(8,128)S(1)}, u32[]{:S(2)}, u32[]{:S(2)}) %collective-permute-start) | collective-permute-done | bytes 65568 | tf_op jit(solution)/shard_map/ppermute | solution.py:30
  8.9 0.2 collective-permute-start.2
  9.1 6.3 %collective-permute-start.4 = (f32[256,128]{1,0:T(8,128)S(1)}, f32[256,128]{1,0:T(8,128)S(1)}, u32[]{:S(2)}, u32[]{:S(2)}) collective-permute-start(f32[256,128]{1,0:T(8,128)S(1)} %slice_select_fusion.panel_ref.refs_1_), channel_id=1, source_target_pairs={{0,1},{1,0},{2,3},{3,2},{4,5},{5,4},{6,7},{7,6},{8,9},{9,8},{10,11... | collective-permute-start | bytes 393224 | tf_op jit(solution)/shard_map/ppermute | solution.py:30
  15.4 4.0 %collective-permute-start.3 = (f32[192,128]{1,0:T(8,128)S(1)}, f32[192,128]{1,0:T(8,128)S(1)}, u32[]{:S(2)}, u32[]{:S(2)}) collective-permute-start(f32[192,128]{1,0:T(8,128)S(1)} %pad_maximum_fusion.5), channel_id=1, source_target_pairs={{0,56},{1,57},{4,60},{5,61},{10,50},{11,51},{14,54},{15,55},{16,40... | collective-permute-start | bytes 294920 | tf_op jit(solution)/shard_map/ppermute | solution.py:30
  19.4 1.7 %collective-permute-done.3 = f32[192,128]{1,0:T(8,128)S(1)} collective-permute-done((f32[192,128]{1,0:T(8,128)S(1)}, f32[192,128]{1,0:T(8,128)S(1)}, u32[]{:S(2)}, u32[]{:S(2)}) %collective-permute-start.3) | collective-permute-done | bytes 98336 | tf_op jit(solution)/shard_map/ppermute | solution.py:30
  21.2 2.2 %collective-permute-start.5 = (f32[192,128]{1,0:T(8,128)S(1)}, f32[192,128]{1,0:T(8,128)S(1)}, u32[]{:S(2)}, u32[]{:S(2)}) collective-permute-start(f32[192,128]{1,0:T(8,128)S(1)} %pad_maximum_fusion.6), channel_id=1, source_target_pairs={{0,16},{1,17},{2,18},{3,19},{4,20},{5,21},{6,22},{7,23},{8,24},{9,... | collective-permute-start | bytes 294920 | tf_op jit(solution)/shard_map/ppermute | solution.py:30
  23.4 2.3 %collective-permute-done.5 = f32[192,128]{1,0:T(8,128)S(1)} collective-permute-done((f32[192,128]{1,0:T(8,128)S(1)}, f32[192,128]{1,0:T(8,128)S(1)}, u32[]{:S(2)}, u32[]{:S(2)}) %collective-permute-start.5) | collective-permute-done | bytes 98336 | tf_op jit(solution)/shard_map/ppermute | solution.py:30
  25.7 1.4 %collective-permute-start.6 = (f32[320,128]{1,0:T(8,128)S(1)}, f32[320,128]{1,0:T(8,128)S(1)}, u32[]{:S(2)}, u32[]{:S(2)}) collective-permute-start(f32[320,128]{1,0:T(8,128)S(1)} %pad_maximum_fusion.3), channel_id=1, source_target_pairs={{0,8},{1,9},{2,10},{3,11},{4,12},{5,13},{6,14},{7,15},{8,0},{9,1},... | collective-permute-start | bytes 491528 | tf_op jit(solution)/shard_map/ppermute | solution.py:30
  27.2 3.2 %collective-permute-done.6 = f32[320,128]{1,0:T(8,128)S(1)} collective-permute-done((f32[320,128]{1,0:T(8,128)S(1)}, f32[320,128]{1,0:T(8,128)S(1)}, u32[]{:S(2)}, u32[]{:S(2)}) %collective-permute-start.6) | collective-permute-done | bytes 163872 | tf_op jit(solution)/shard_map/ppermute | solution.py:30
  30.5 2.6 %collective-permute-start.8 = (f32[576,128]{1,0:T(8,128)S(1)}, f32[576,128]{1,0:T(8,128)S(1)}, u32[]{:S(2)}, u32[]{:S(2)}) collective-permute-start(f32[576,128]{1,0:T(8,128)S(1)} %pad_maximum_fusion), channel_id=1, source_target_pairs={{0,192},{1,193},{2,194},{3,195},{4,196},{5,197},{6,198},{7,199},{8... | collective-permute-start | bytes 884744 | tf_op jit(solution)/shard_map/ppermute | solution.py:30
  33.0 2.3 %collective-permute-start.9 = (f32[256,128]{1,0:T(8,128)S(1)}, f32[256,128]{1,0:T(8,128)S(1)}, u32[]{:S(2)}, u32[]{:S(2)}) collective-permute-start(f32[256,128]{1,0:T(8,128)S(1)} %shard_map.18), channel_id=1, source_target_pairs={{0,3},{1,2},{2,1},{3,0},{4,7},{5,6},{6,5},{7,4},{8,11},{9,10},{10,... | collective-permute-start | bytes 393224 | tf_op jit(solution)/shard_map/ppermute | solution.py:30
  35.3 4.3 %collective-permute-start.10 = (f32[512,128]{1,0:T(8,128)S(1)}, f32[512,128]{1,0:T(8,128)S(1)}, u32[]{:S(2)}, u32[]{:S(2)}) collective-permute-start(f32[512,128]{1,0:T(8,128)S(1)} %pad_maximum_fusion.2.refs_4_), channel_id=1, source_target_pairs={{0,4},{1,5},{2,6},{3,7},{4,0},{5,1},{6,2},{7,3},{8,12},{9,13},{10,... | collective-permute-start | bytes 786440 | tf_op jit(solution)/shard_map/ppermute | solution.py:30
  39.7 5.1 %collective-permute-start.14 = (f32[512,128]{1,0:T(8,128)S(1)}, f32[512,128]{1,0:T(8,128)S(1)}, u32[]{:S(2)}, u32[]{:S(2)}) collective-permute-start(f32[512,128]{1,0:T(8,128)S(1)} %slice.78), channel_id=1, source_target_pairs={{0,4},{1,5},{2,6},{3,7},{4,0},{5,1},{6,2},{7,3},{8,12},{9,13},{10,... | collective-permute-start | bytes 786440 | tf_op jit(solution)/shard_map/ppermute | solution.py:30
  44.8 0.1 collective-permute-start.11
  45.0 1.4 %collective-permute-start.12 = (f32[320,128]{1,0:T(8,128)S(1)}, f32[320,128]{1,0:T(8,128)S(1)}, u32[]{:S(2)}, u32[]{:S(2)}) collective-permute-start(f32[320,128]{1,0:T(8,128)S(1)} %pad_maximum_fusion.4), channel_id=1, source_target_pairs={{0,64},{1,65},{2,66},{3,67},{4,68},{5,69},{6,70},{7,71},{8,72},{9,... | collective-permute-start | bytes 491528 | tf_op jit(solution)/shard_map/ppermute | solution.py:30
  46.4 0.5 collective-permute-start.13
  46.9 2.2 %copy-done = f32[256,4096]{1,0:T(8,128)S(1)} copy-done((f32[256,4096]{1,0:T(8,128)S(1)}, f32[256,4096]{1,0:T(8,128)}, u32[]{:S(2)}) %copy-start) | copy-done | bytes 4194328
  49.1 3.4 %shard_map.19.refs_14_ = f32[256,4096]{1,0:T(8,128)} custom-call(f32[256,4096]{1,0:T(8,128)S(1)} %copy-done, f32[256,128]{1,0:T(8,128)S(1)} %slice_select_fusion.panel_ref.refs_1_, f32[256,128]{1,0:T(8,128)S(1)} %collective-permute-done.4.rows_ref.refs_2_, f32[256,128]{1,0:T(8,128)S(1)} %collective-permute-done.9.refs_3_, ...), custom_call_target="tpu_custom_call" | custom-call | flops 805306368 | bytes 6291456 | tf_op jit(solution)/shard_map/pallas_call | solution.py:239
  52.6 1.4 %collective-permute-start.15 = (f32[576,128]{1,0:T(8,128)S(1)}, f32[576,128]{1,0:T(8,128)S(1)}, u32[]{:S(2)}, u32[]{:S(2)}) collective-permute-start(f32[576,128]{1,0:T(8,128)S(1)} %pad_maximum_fusion.1.refs_8_), channel_id=1, source_target_pairs={{0,4},{1,5},{2,6},{3,7},{4,0},{5,1},{6,2},{7,3},{8,12},{9,13},{10,... | collective-permute-start | bytes 884744 | tf_op jit(solution)/shard_map/ppermute | solution.py:30
  53.9 1.2 %collective-permute-done.15.refs_9_ = f32[576,128]{1,0:T(8,128)S(1)} collective-permute-done((f32[576,128]{1,0:T(8,128)S(1)}, f32[576,128]{1,0:T(8,128)S(1)}, u32[]{:S(2)}, u32[]{:S(2)}) %collective-permute-start.15) | collective-permute-done | bytes 294944 | tf_op jit(solution)/shard_map/ppermute | solution.py:30
  55.2 2.0 %shard_map.20 = f32[256,4096]{1,0:T(8,128)} custom-call(f32[256,4096]{1,0:T(8,128)S(1)} %copy-done, f32[256,128]{1,0:T(8,128)S(1)} %slice_select_fusion.panel_ref.refs_1_, f32[256,128]{1,0:T(8,128)S(1)} %collective-permute-done.4.rows_ref.refs_2_, f32[256,128]{1,0:T(8,128)S(1)} %collective-permute-done.9.refs_3_, ...), custom_call_target="tpu_custom_call", output_to_operand_aliasing={{}: (14, {})} | custom-call | flops 268435456 | bytes 2097152 | tf_op jit(solution)/shard_map/pallas_call | solution.py:239
  (42 shorter events, 0.4 us)
Async XLA Ops:
  1.0 6.5 %collective-permute-start.1 = (f32[128,128]{1,0:T(8,128)S(1)}, f32[128,128]{1,0:T(8,128)S(1)}, u32[]{:S(2)}, u32[]{:S(2)}) collective-permute-start(f32[128,128]{1,0:T(8,128)S(1)} %get-tuple-element.29), channel_id=1, source_target_pairs={{0,0},{4,1},{8,10},{12,11},{16,16},{20,17},{24,26},{28,27},{32,32}... | collective-permute-start | bytes 196616 | tf_op jit(solution)/shard_map/ppermute | solution.py:30
  5.6 3.2 %collective-permute-start = (f32[128,128]{1,0:T(8,128)S(1)}, f32[128,128]{1,0:T(8,128)S(1)}, u32[]{:S(2)}, u32[]{:S(2)}) collective-permute-start(f32[128,128]{1,0:T(8,128)S(1)} %get-tuple-element.30.a_ref), channel_id=1, source_target_pairs={{0,4},{4,5},{8,14},{12,15},{16,20},{20,21},{24,30},{28,31},{32,36}... | collective-permute-start | bytes 196616 | tf_op jit(solution)/shard_map/ppermute | solution.py:30
  8.9 6.4 %collective-permute-start.2 = (f32[64,128]{1,0:T(8,128)S(1)}, f32[64,128]{1,0:T(8,128)S(1)}, u32[]{:S(2)}, u32[]{:S(2)}) collective-permute-start(f32[64,128]{1,0:T(8,128)S(1)} %slice.67), channel_id=1, source_target_pairs={{0,4},{1,5},{2,6},{3,7},{4,0},{5,1},{6,2},{7,3},{8,12},{9,13},{10,... | collective-permute-start | bytes 98312 | tf_op jit(solution)/shard_map/ppermute | solution.py:30
  9.1 12.1 %collective-permute-start.4 = (f32[256,128]{1,0:T(8,128)S(1)}, f32[256,128]{1,0:T(8,128)S(1)}, u32[]{:S(2)}, u32[]{:S(2)}) collective-permute-start(f32[256,128]{1,0:T(8,128)S(1)} %slice_select_fusion.panel_ref.refs_1_), channel_id=1, source_target_pairs={{0,1},{1,0},{2,3},{3,2},{4,5},{5,4},{6,7},{7,6},{8,9},{9,8},{10,11... | collective-permute-start | bytes 393224 | tf_op jit(solution)/shard_map/ppermute | solution.py:30
  15.4 5.8 %collective-permute-start.3 = (f32[192,128]{1,0:T(8,128)S(1)}, f32[192,128]{1,0:T(8,128)S(1)}, u32[]{:S(2)}, u32[]{:S(2)}) collective-permute-start(f32[192,128]{1,0:T(8,128)S(1)} %pad_maximum_fusion.5), channel_id=1, source_target_pairs={{0,56},{1,57},{4,60},{5,61},{10,50},{11,51},{14,54},{15,55},{16,40... | collective-permute-start | bytes 294920 | tf_op jit(solution)/shard_map/ppermute | solution.py:30
  21.2 4.5 %collective-permute-start.5 = (f32[192,128]{1,0:T(8,128)S(1)}, f32[192,128]{1,0:T(8,128)S(1)}, u32[]{:S(2)}, u32[]{:S(2)}) collective-permute-start(f32[192,128]{1,0:T(8,128)S(1)} %pad_maximum_fusion.6), channel_id=1, source_target_pairs={{0,16},{1,17},{2,18},{3,19},{4,20},{5,21},{6,22},{7,23},{8,24},{9,... | collective-permute-start | bytes 294920 | tf_op jit(solution)/shard_map/ppermute | solution.py:30
  25.7 4.7 %collective-permute-start.6 = (f32[320,128]{1,0:T(8,128)S(1)}, f32[320,128]{1,0:T(8,128)S(1)}, u32[]{:S(2)}, u32[]{:S(2)}) collective-permute-start(f32[320,128]{1,0:T(8,128)S(1)} %pad_maximum_fusion.3), channel_id=1, source_target_pairs={{0,8},{1,9},{2,10},{3,11},{4,12},{5,13},{6,14},{7,15},{8,0},{9,1},... | collective-permute-start | bytes 491528 | tf_op jit(solution)/shard_map/ppermute | solution.py:30
  30.5 9.2 %collective-permute-start.8 = (f32[576,128]{1,0:T(8,128)S(1)}, f32[576,128]{1,0:T(8,128)S(1)}, u32[]{:S(2)}, u32[]{:S(2)}) collective-permute-start(f32[576,128]{1,0:T(8,128)S(1)} %pad_maximum_fusion), channel_id=1, source_target_pairs={{0,192},{1,193},{2,194},{3,195},{4,196},{5,197},{6,198},{7,199},{8... | collective-permute-start | bytes 884744 | tf_op jit(solution)/shard_map/ppermute | solution.py:30
  33.0 6.6 %collective-permute-start.7 = (f32[576,128]{1,0:T(8,128)S(1)}, f32[576,128]{1,0:T(8,128)S(1)}, u32[]{:S(2)}, u32[]{:S(2)}) collective-permute-start(f32[576,128]{1,0:T(8,128)S(1)} %pad_maximum_fusion), channel_id=1, source_target_pairs={{0,64},{1,65},{2,66},{3,67},{4,68},{5,69},{6,70},{7,71},{8,72},{9,... | collective-permute-start | bytes 884744 | tf_op jit(solution)/shard_map/ppermute | solution.py:30
  33.0 6.6 %collective-permute-start.9 = (f32[256,128]{1,0:T(8,128)S(1)}, f32[256,128]{1,0:T(8,128)S(1)}, u32[]{:S(2)}, u32[]{:S(2)}) collective-permute-start(f32[256,128]{1,0:T(8,128)S(1)} %shard_map.18), channel_id=1, source_target_pairs={{0,3},{1,2},{2,1},{3,0},{4,7},{5,6},{6,5},{7,4},{8,11},{9,10},{10,... | collective-permute-start | bytes 393224 | tf_op jit(solution)/shard_map/ppermute | solution.py:30
  35.3 11.5 %collective-permute-start.10 = (f32[512,128]{1,0:T(8,128)S(1)}, f32[512,128]{1,0:T(8,128)S(1)}, u32[]{:S(2)}, u32[]{:S(2)}) collective-permute-start(f32[512,128]{1,0:T(8,128)S(1)} %pad_maximum_fusion.2.refs_4_), channel_id=1, source_target_pairs={{0,4},{1,5},{2,6},{3,7},{4,0},{5,1},{6,2},{7,3},{8,12},{9,13},{10,... | collective-permute-start | bytes 786440 | tf_op jit(solution)/shard_map/ppermute | solution.py:30
  39.7 7.2 %collective-permute-start.14 = (f32[512,128]{1,0:T(8,128)S(1)}, f32[512,128]{1,0:T(8,128)S(1)}, u32[]{:S(2)}, u32[]{:S(2)}) collective-permute-start(f32[512,128]{1,0:T(8,128)S(1)} %slice.78), channel_id=1, source_target_pairs={{0,4},{1,5},{2,6},{3,7},{4,0},{5,1},{6,2},{7,3},{8,12},{9,13},{10,... | collective-permute-start | bytes 786440 | tf_op jit(solution)/shard_map/ppermute | solution.py:30
  44.8 2.0 %collective-permute-start.11 = (f32[512,128]{1,0:T(8,128)S(1)}, f32[512,128]{1,0:T(8,128)S(1)}, u32[]{:S(2)}, u32[]{:S(2)}) collective-permute-start(f32[512,128]{1,0:T(8,128)S(1)} %slice.74), channel_id=1, source_target_pairs={{0,4},{1,5},{2,6},{3,7},{4,0},{5,1},{6,2},{7,3},{8,12},{9,13},{10,... | collective-permute-start | bytes 786440 | tf_op jit(solution)/shard_map/ppermute | solution.py:30
  45.0 7.5 %collective-permute-start.12 = (f32[320,128]{1,0:T(8,128)S(1)}, f32[320,128]{1,0:T(8,128)S(1)}, u32[]{:S(2)}, u32[]{:S(2)}) collective-permute-start(f32[320,128]{1,0:T(8,128)S(1)} %pad_maximum_fusion.4), channel_id=1, source_target_pairs={{0,64},{1,65},{2,66},{3,67},{4,68},{5,69},{6,70},{7,71},{8,72},{9,... | collective-permute-start | bytes 491528 | tf_op jit(solution)/shard_map/ppermute | solution.py:30
  46.4 6.1 %collective-permute-start.13 = (f32[256,128]{1,0:T(8,128)S(1)}, f32[256,128]{1,0:T(8,128)S(1)}, u32[]{:S(2)}, u32[]{:S(2)}) collective-permute-start(f32[256,128]{1,0:T(8,128)S(1)} %slice.77), channel_id=1, source_target_pairs={{0,192},{1,193},{2,194},{3,195},{4,196},{5,197},{6,198},{7,199},{8... | collective-permute-start | bytes 393224 | tf_op jit(solution)/shard_map/ppermute | solution.py:30
  46.9 2.2 %copy-start = (f32[256,4096]{1,0:T(8,128)S(1)}, f32[256,4096]{1,0:T(8,128)}, u32[]{:S(2)}) copy-start(f32[256,4096]{1,0:T(8,128)} %refs_0_.3) | copy-start | bytes 12582916
  52.6 2.6 %collective-permute-start.15 = (f32[576,128]{1,0:T(8,128)S(1)}, f32[576,128]{1,0:T(8,128)S(1)}, u32[]{:S(2)}, u32[]{:S(2)}) collective-permute-start(f32[576,128]{1,0:T(8,128)S(1)} %pad_maximum_fusion.1.refs_8_), channel_id=1, source_target_pairs={{0,4},{1,5},{2,6},{3,7},{4,0},{5,1},{6,2},{7,3},{8,12},{9,13},{10,... | collective-permute-start | bytes 884744 | tf_op jit(solution)/shard_map/ppermute | solution.py:30

commit v4 on v3

--- a/solution.py
+++ b/solution.py
@@ -113,19 +113,30 @@
     out_ref[...] = jnp.where(y == 1, rows_ref[...], panel_ref[...])
 
 
-def panels(y, p_ref):
-    p = jnp.where(y == 0, p_ref[0][...], jnp.where(y == 1, p_ref[1][...], p_ref[2][...]))
-    hi, lo = split(p)
+def rows_kernel(panel_ref, rows_a_ref, rows_b_ref, out_ref):
+    x, z, core, y, row = place()
+    later = jnp.where(y == 1, rows_a_ref[...], rows_b_ref[...])
+    out_ref[...] = jnp.where(y == 0, panel_ref[...], later)
+
+
+def stage_kernel(a_ref, out_ref, sem):
+    copy = pltpu.make_async_copy(a_ref, out_ref, sem)
+    copy.start()
+    copy.wait()
+
+
+def panels(p_ref):
+    hi, lo = split(p_ref[...])
     return hi, jnp.concatenate([hi, lo], axis=1)
 
 
-def update_kernel(hops, last, a_ref, *refs):
-    p_refs, refs = refs[:3], refs[3:]
+def update_kernel(hops, last, aliased, a_ref, *refs):
+    p_ref, refs = refs[0], refs[1:]
     count = 8 if last else 2 * len(hops)
     pieces, refs = refs[:count], refs[count:]
     if last:
         low_ref, inv_ref, refs = refs[0], refs[1], refs[2:]
-    if hops[0] != 0:
+    if aliased:
         refs = refs[1:]
     out_ref, a_buf, o_buf, in_sem, out_sem = refs[:5]
     x, z, core, y, row = place()
@@ -146,7 +157,7 @@
         col_buf, res_buf, piece_buf, col_sem, res_sem = refs[5:]
         col_in = pltpu.make_async_copy(a_ref.at[:, :NB], col_buf, col_sem)
         col_in.start()
-    hi, both = panels(y, p_refs)
+    hi, both = panels(p_ref)
 
     special = y == 1
     if last:
@@ -207,12 +218,13 @@
     return pl.BlockSpec(memory_space=pltpu.VMEM)
 
 
-def update(hops, matrix, cands, pieces, out=None, factors=()):
+def update(hops, matrix, rows, pieces, out=None, factors=()):
     last = len(factors) > 0
     groups = 2 * len(hops)
     hbm = pl.BlockSpec(memory_space=pltpu.HBM)
-    args = [matrix, *cands, *pieces, *factors]
-    specs = [hbm] + [vmem()] * (len(args) - 1)
+    free = pl.BlockSpec(memory_space=pl.ANY)
+    args = [matrix, rows, *pieces, *factors]
+    specs = [free] + [vmem()] * (len(args) - 1)
     alias = {}
     if out is not None:
         alias = {len(args): 0}
@@ -234,7 +246,7 @@
         ]
 
     def kernel(*refs):
-        update_kernel(hops, last, *refs)
+        update_kernel(hops, last, out is not None, *refs)
 
     return pl.pallas_call(
         kernel,
@@ -311,29 +323,51 @@
         ),
     )(panel, rows_a)
     rows_b = move(forward, lambda X, Y, Z, C: (X, Y ^ 3, Z, C))
-    near_a, near_b, rows_b = lax.optimization_barrier((near_a, near_b, rows_b))
-    cands = [panel, rows_a, rows_b]
+    staged = pl.pallas_call(
+        stage_kernel,
+        out_shape=jax.ShapeDtypeStruct(matrix.shape, jnp.float32),
+        in_specs=[pl.BlockSpec(memory_space=pl.ANY)],
+        out_specs=pl.BlockSpec(memory_space=pl.ANY),
+        scratch_shapes=[pltpu.SemaphoreType.DMA],
+        compiler_params=pltpu.CompilerParams(vmem_limit_bytes=8 * MIB),
+        cost_estimate=pl.CostEstimate(
+            flops=5 * 10**9, bytes_accessed=8 * MIB, transcendentals=0
+        ),
+    )(matrix)
+    near_a, near_b, rows_b, four_o, staged = lax.optimization_barrier(
+        (near_a, near_b, rows_b, four_o, staged)
+    )
+    rows = pl.pallas_call(
+        rows_kernel,
+        out_shape=jax.ShapeDtypeStruct(panel.shape, jnp.float32),
+        in_specs=[vmem(), vmem(), vmem()],
+        out_specs=vmem(),
+        compiler_params=pltpu.CompilerParams(vmem_limit_bytes=8 * MIB),
+        cost_estimate=pl.CostEstimate(
+            flops=5 * 10**9, bytes_accessed=8 * NB * NB * 4, transcendentals=0
+        ),
+    )(panel, rows_a, rows_b)
     far_a = move(
         jnp.concatenate([near_b[: 2 * NB], near_b[4 * NB :]]),
         lambda X, Y, Z, C: (X ^ 1, Y, Z, C),
     )
     far_b = move(near_a[2 * NB : 4 * NB], lambda X, Y, Z, C: (X ^ 3, Y, Z, C))
     near_a_o, near_b_o = move(near_a[: 4 * NB], other), move(near_b[: 4 * NB], other)
-    near = [four, four_o, near_a, near_a_o, near_b, near_b_o]
-    out = update((0, 1, 3), matrix, cands, near)
+    out = update((1, 3), staged, rows, [near_a, near_a_o, near_b, near_b_o])
     far_a, far_b, out = lax.optimization_barrier((far_a, far_b, out))
     seed = jnp.where(x == 1, near_a[4 * NB :], seed)
     seed = jnp.where(x == 3, near_b[4 * NB :], seed)
     seed = jnp.where(x == 2, far_a[2 * NB :], seed)
     far = jnp.concatenate([far_a[: 2 * NB], far_b, seed])
     far_o = move(far, other)
+    out = update((0,), staged, rows, [four, four_o], out)
     inverse = jnp.where(
         core == 1,
         jnp.concatenate([far_o[4 * NB :], seed]),
         jnp.concatenate([seed, far_o[4 * NB :]]),
     )
     pieces = [four, four_o, near_a, near_a_o, far, far_o, near_b, near_b_o]
-    return update((2,), matrix, cands, pieces, out, (lower, inverse))
+    return update((2,), staged, rows, pieces, out, (lower, inverse))
 
 
 def solution(mesh):

time: 57.5 us -> 55.8 us (0.970)
  starting transfers between devices: 38.1 us -> 36.7 us
  waiting for transfers between devices: 9.82 us -> 8.45 us
  Pallas kernels: 5.46 us -> 6.62 us
    ppermute x16, starting transfers between devices: 38.1 us -> 36.7 us  [move(): return lax.ppermute(block, AXES, pairs)]
    ppermute x16, waiting for transfers between devices: 9.82 us -> 8.45 us  [move(): return lax.ppermute(block, AXES, pairs)]
    pallas_call x2 -> x3, Pallas kernels: 5.41 us -> 6.26 us  [update(): pl.pallas_call(kernel, out_shape=jax.ShapeDtypeStruct(matrix.shape, jnp.f...]
    unnamed x2 -> x6, local copies, waits for them, and re-layouts: 2.18 us -> 2.02 us
  transfers between devices with their start and end apart: 16 -> 16, of which waited for: 5 -> 6; matrix products, arithmetic and copies ran while one was open for 0% -> 0% of each run, Pallas kernels for 6% -> 8%
where the time goes in v4:
time: 55.8 us; the launch traced here: 55.6 us
  starting transfers between devices  36.7 us (66%)
  waiting for transfers between devices  8.45 us (15%)
  Pallas kernels  6.62 us (12%)
  local copies, waits for them, and re-layouts  2.13 us (4%)
  other arithmetic  1.18 us (2%)
  between operations  0.56 us (1%)
    ppermute x16, starting transfers between devices, move(): return lax.ppermute(block, AXES, pairs)  36.7 us
    ppermute x16, waiting for transfers between devices, move(): return lax.ppermute(block, AXES, pairs)  8.45 us
    pallas_call x3, Pallas kernels, update(): pl.pallas_call(kernel, out_shape=jax.ShapeDtypeStruct(matrix.shape, jnp.f...  6.26 us
    unnamed x6, local copies, waits for them, and re-layouts  2.02 us
  transfers between devices with their start and end apart: 16, of which 6 were waited for; matrix products, arithmetic and copies ran while one was open for 0% of the time, Pallas kernels for 8%

profile of v4, /device:TPU:1, one launch (start us, length us, event | category | flops | bytes accessed | tf_op | source)
XLA Modules:
  0.0 55.6 jit_solution(5741477716899082275)
XLA Ops:
  0.0 1.0 %slice_select_fusion.panel_ref = f32[256,128]{1,0:T(8,128)S(1)} fusion(f32[256,4096]{1,0:T(8,128)} %a_ref.1, pred[256]{0:T(512)(128)(4,1)S(1)} %compare_or_fusion), kind=kLoop, calls=%fused_computation.5 | loop fusion | flops 32768 | bytes 262400 | tf_op jit(solution)/shard_map/jit(_where)/select_n | solution.py:272
  1.0 4.6 %collective-permute-start.1 = (f32[128,128]{1,0:T(8,128)S(1)}, f32[128,128]{1,0:T(8,128)S(1)}, u32[]{:S(2)}, u32[]{:S(2)}) collective-permute-start(f32[128,128]{1,0:T(8,128)S(1)} %get-tuple-element.33), channel_id=1, source_target_pairs={{0,0},{4,1},{8,10},{12,11},{16,16},{20,17},{24,26},{28,27},{32,32}... | collective-permute-start | bytes 196616 | tf_op jit(solution)/shard_map/ppermute | solution.py:30
  5.6 1.9 %collective-permute-start = (f32[128,128]{1,0:T(8,128)S(1)}, f32[128,128]{1,0:T(8,128)S(1)}, u32[]{:S(2)}, u32[]{:S(2)}) collective-permute-start(f32[128,128]{1,0:T(8,128)S(1)} %get-tuple-element.34.a_ref), channel_id=1, source_target_pairs={{0,4},{4,5},{8,14},{12,15},{16,20},{20,21},{24,30},{28,31},{32,36}... | collective-permute-start | bytes 196616 | tf_op jit(solution)/shard_map/ppermute | solution.py:30
  7.6 1.3 %collective-permute-done = f32[128,128]{1,0:T(8,128)S(1)} collective-permute-done((f32[128,128]{1,0:T(8,128)S(1)}, f32[128,128]{1,0:T(8,128)S(1)}, u32[]{:S(2)}, u32[]{:S(2)}) %collective-permute-start) | collective-permute-done | bytes 65568 | tf_op jit(solution)/shard_map/ppermute | solution.py:30
  9.1 6.3 %collective-permute-start.4 = (f32[256,128]{1,0:T(8,128)S(1)}, f32[256,128]{1,0:T(8,128)S(1)}, u32[]{:S(2)}, u32[]{:S(2)}) collective-permute-start(f32[256,128]{1,0:T(8,128)S(1)} %slice_select_fusion.panel_ref), channel_id=1, source_target_pairs={{0,1},{1,0},{2,3},{3,2},{4,5},{5,4},{6,7},{7,6},{8,9},{9,8},{10,11... | collective-permute-start | bytes 393224 | tf_op jit(solution)/shard_map/ppermute | solution.py:30
  15.4 4.0 %collective-permute-start.3 = (f32[192,128]{1,0:T(8,128)S(1)}, f32[192,128]{1,0:T(8,128)S(1)}, u32[]{:S(2)}, u32[]{:S(2)}) collective-permute-start(f32[192,128]{1,0:T(8,128)S(1)} %pad_maximum_fusion.5), channel_id=1, source_target_pairs={{0,56},{1,57},{4,60},{5,61},{10,50},{11,51},{14,54},{15,55},{16,40... | collective-permute-start | bytes 294920 | tf_op jit(solution)/shard_map/ppermute | solution.py:30
  19.4 1.7 %collective-permute-done.3 = f32[192,128]{1,0:T(8,128)S(1)} collective-permute-done((f32[192,128]{1,0:T(8,128)S(1)}, f32[192,128]{1,0:T(8,128)S(1)}, u32[]{:S(2)}, u32[]{:S(2)}) %collective-permute-start.3) | collective-permute-done | bytes 98336 | tf_op jit(solution)/shard_map/ppermute | solution.py:30
  21.2 2.2 %collective-permute-start.5 = (f32[192,128]{1,0:T(8,128)S(1)}, f32[192,128]{1,0:T(8,128)S(1)}, u32[]{:S(2)}, u32[]{:S(2)}) collective-permute-start(f32[192,128]{1,0:T(8,128)S(1)} %pad_maximum_fusion.6), channel_id=1, source_target_pairs={{0,16},{1,17},{2,18},{3,19},{4,20},{5,21},{6,22},{7,23},{8,24},{9,... | collective-permute-start | bytes 294920 | tf_op jit(solution)/shard_map/ppermute | solution.py:30
  23.4 2.3 %collective-permute-done.5 = f32[192,128]{1,0:T(8,128)S(1)} collective-permute-done((f32[192,128]{1,0:T(8,128)S(1)}, f32[192,128]{1,0:T(8,128)S(1)}, u32[]{:S(2)}, u32[]{:S(2)}) %collective-permute-start.5) | collective-permute-done | bytes 98336 | tf_op jit(solution)/shard_map/ppermute | solution.py:30
  25.7 1.4 %collective-permute-start.6 = (f32[320,128]{1,0:T(8,128)S(1)}, f32[320,128]{1,0:T(8,128)S(1)}, u32[]{:S(2)}, u32[]{:S(2)}) collective-permute-start(f32[320,128]{1,0:T(8,128)S(1)} %pad_maximum_fusion.3), channel_id=1, source_target_pairs={{0,8},{1,9},{2,10},{3,11},{4,12},{5,13},{6,14},{7,15},{8,0},{9,1},... | collective-permute-start | bytes 491528 | tf_op jit(solution)/shard_map/ppermute | solution.py:30
  27.2 1.4 %collective-permute-start.9 = (f32[256,128]{1,0:T(8,128)S(1)}, f32[256,128]{1,0:T(8,128)S(1)}, u32[]{:S(2)}, u32[]{:S(2)}) collective-permute-start(f32[256,128]{1,0:T(8,128)S(1)} %shard_map.18), channel_id=1, source_target_pairs={{0,3},{1,2},{2,1},{3,0},{4,7},{5,6},{6,5},{7,4},{8,11},{9,10},{10,... | collective-permute-start | bytes 393224 | tf_op jit(solution)/shard_map/ppermute | solution.py:30
  28.6 1.9 %collective-permute-done.6 = f32[320,128]{1,0:T(8,128)S(1)} collective-permute-done((f32[320,128]{1,0:T(8,128)S(1)}, f32[320,128]{1,0:T(8,128)S(1)}, u32[]{:S(2)}, u32[]{:S(2)}) %collective-permute-start.6) | collective-permute-done | bytes 163872 | tf_op jit(solution)/shard_map/ppermute | solution.py:30
  30.5 2.6 %collective-permute-start.8 = (f32[576,128]{1,0:T(8,128)S(1)}, f32[576,128]{1,0:T(8,128)S(1)}, u32[]{:S(2)}, u32[]{:S(2)}) collective-permute-start(f32[576,128]{1,0:T(8,128)S(1)} %pad_maximum_fusion), channel_id=1, source_target_pairs={{0,192},{1,193},{2,194},{3,195},{4,196},{5,197},{6,198},{7,199},{8... | collective-permute-start | bytes 884744 | tf_op jit(solution)/shard_map/ppermute | solution.py:30
  33.1 5.2 %collective-permute-start.10 = (f32[512,128]{1,0:T(8,128)S(1)}, f32[512,128]{1,0:T(8,128)S(1)}, u32[]{:S(2)}, u32[]{:S(2)}) collective-permute-start(f32[512,128]{1,0:T(8,128)S(1)} %pad_maximum_fusion.2.refs_2_), channel_id=1, source_target_pairs={{0,4},{1,5},{2,6},{3,7},{4,0},{5,1},{6,2},{7,3},{8,12},{9,13},{10,... | collective-permute-start | bytes 786440 | tf_op jit(solution)/shard_map/ppermute | solution.py:30
  38.5 2.0 %copy-done = f32[256,4096]{1,0:T(8,128)} copy-done((f32[256,4096]{1,0:T(8,128)}, f32[256,4096]{1,0:T(8,128)S(1)}, u32[]{:S(2)}) %copy-start) | copy-done | bytes 4194328
  40.7 0.9 %collective-permute-start.13 = (f32[256,128]{1,0:T(8,128)S(1)}, f32[256,128]{1,0:T(8,128)S(1)}, u32[]{:S(2)}, u32[]{:S(2)}) collective-permute-start(f32[256,128]{1,0:T(8,128)S(1)} %slice.77), channel_id=1, source_target_pairs={{0,192},{1,193},{2,194},{3,195},{4,196},{5,197},{6,198},{7,199},{8... | collective-permute-start | bytes 393224 | tf_op jit(solution)/shard_map/ppermute | solution.py:30
  41.6 0.8 %collective-permute-start.12 = (f32[320,128]{1,0:T(8,128)S(1)}, f32[320,128]{1,0:T(8,128)S(1)}, u32[]{:S(2)}, u32[]{:S(2)}) collective-permute-start(f32[320,128]{1,0:T(8,128)S(1)} %pad_maximum_fusion.4), channel_id=1, source_target_pairs={{0,64},{1,65},{2,66},{3,67},{4,68},{5,69},{6,70},{7,71},{8,72},{9,... | collective-permute-start | bytes 491528 | tf_op jit(solution)/shard_map/ppermute | solution.py:30
  42.4 3.9 %collective-permute-start.14 = (f32[512,128]{1,0:T(8,128)S(1)}, f32[512,128]{1,0:T(8,128)S(1)}, u32[]{:S(2)}, u32[]{:S(2)}) collective-permute-start(f32[512,128]{1,0:T(8,128)S(1)} %slice.78), channel_id=1, source_target_pairs={{0,4},{1,5},{2,6},{3,7},{4,0},{5,1},{6,2},{7,3},{8,12},{9,13},{10,... | collective-permute-start | bytes 786440 | tf_op jit(solution)/shard_map/ppermute | solution.py:30
  46.6 0.9 %collective-permute-done.14.refs_5_.refs_9_ = f32[512,128]{1,0:T(8,128)S(1)} collective-permute-done((f32[512,128]{1,0:T(8,128)S(1)}, f32[512,128]{1,0:T(8,128)S(1)}, u32[]{:S(2)}, u32[]{:S(2)}) %collective-permute-start.14) | collective-permute-done | bytes 262176 | tf_op jit(solution)/shard_map/ppermute | solution.py:30
  47.5 0.4 collective-permute-done.11.refs_3_.refs_5_
  47.9 2.6 %shard_map.21.refs_4_ = f32[256,4096]{1,0:T(8,128)} custom-call(f32[256,4096]{1,0:T(8,128)S(1)} %copy-done.1, f32[256,128]{1,0:T(8,128)S(1)} %shard_map.20.refs_1_, f32[576,128]{1,0:T(8,128)S(1)} %collective-permute-done.7.refs_2_.refs_4_, f32[512,128]{1,0:T(8,128)S(1)} %collective-permute-done.11.refs_3_.refs_5_, ...), custom_call_target="tpu_custom_call" | custom-call | flops 536870912 | bytes 4194304 | tf_op jit(solution)/shard_map/pallas_call | solution.py:251
  50.5 1.2 %collective-permute-start.15 = (f32[576,128]{1,0:T(8,128)S(1)}, f32[576,128]{1,0:T(8,128)S(1)}, u32[]{:S(2)}, u32[]{:S(2)}) collective-permute-start(f32[576,128]{1,0:T(8,128)S(1)} %pad_maximum_fusion.1.refs_6_), channel_id=1, source_target_pairs={{0,4},{1,5},{2,6},{3,7},{4,0},{5,1},{6,2},{7,3},{8,12},{9,13},{10,... | collective-permute-start | bytes 884744 | tf_op jit(solution)/shard_map/ppermute | solution.py:30
  51.7 1.7 %shard_map.22.refs_12_ = f32[256,4096]{1,0:T(8,128)} custom-call(f32[256,4096]{1,0:T(8,128)S(1)} %copy-done.1, f32[256,128]{1,0:T(8,128)S(1)} %shard_map.20.refs_1_, f32[512,128]{1,0:T(8,128)S(1)} %pad_maximum_fusion.2.refs_2_, f32[512,128]{1,0:T(8,128)S(1)} %collective-permute-done.10.refs_3_, ...), custom_call_target="tpu_custom_call", output_to_operand_aliasing={{}: (4, {})} | custom-call | flops 268435456 | bytes 2097152 | tf_op jit(solution)/shard_map/pallas_call | solution.py:251
  53.5 2.0 %shard_map.23 = f32[256,4096]{1,0:T(8,128)} custom-call(f32[256,4096]{1,0:T(8,128)S(1)} %copy-done.1, f32[256,128]{1,0:T(8,128)S(1)} %shard_map.20.refs_1_, f32[512,128]{1,0:T(8,128)S(1)} %pad_maximum_fusion.2.refs_2_, f32[512,128]{1,0:T(8,128)S(1)} %collective-permute-done.10.refs_3_, ...), custom_call_target="tpu_custom_call", output_to_operand_aliasing={{}: (12, {})} | custom-call | flops 268435456 | bytes 2097152 | tf_op jit(solution)/shard_map/pallas_call | solution.py:251
  (49 shorter events, 1.1 us)
Async XLA Ops:
  1.0 6.5 %collective-permute-start.1 = (f32[128,128]{1,0:T(8,128)S(1)}, f32[128,128]{1,0:T(8,128)S(1)}, u32[]{:S(2)}, u32[]{:S(2)}) collective-permute-start(f32[128,128]{1,0:T(8,128)S(1)} %get-tuple-element.33), channel_id=1, source_target_pairs={{0,0},{4,1},{8,10},{12,11},{16,16},{20,17},{24,26},{28,27},{32,32}... | collective-permute-start | bytes 196616 | tf_op jit(solution)/shard_map/ppermute | solution.py:30
  5.6 3.2 %collective-permute-start = (f32[128,128]{1,0:T(8,128)S(1)}, f32[128,128]{1,0:T(8,128)S(1)}, u32[]{:S(2)}, u32[]{:S(2)}) collective-permute-start(f32[128,128]{1,0:T(8,128)S(1)} %get-tuple-element.34.a_ref), channel_id=1, source_target_pairs={{0,4},{4,5},{8,14},{12,15},{16,20},{20,21},{24,30},{28,31},{32,36}... | collective-permute-start | bytes 196616 | tf_op jit(solution)/shard_map/ppermute | solution.py:30
  8.9 6.4 %collective-permute-start.2 = (f32[64,128]{1,0:T(8,128)S(1)}, f32[64,128]{1,0:T(8,128)S(1)}, u32[]{:S(2)}, u32[]{:S(2)}) collective-permute-start(f32[64,128]{1,0:T(8,128)S(1)} %slice.67), channel_id=1, source_target_pairs={{0,4},{1,5},{2,6},{3,7},{4,0},{5,1},{6,2},{7,3},{8,12},{9,13},{10,... | collective-permute-start | bytes 98312 | tf_op jit(solution)/shard_map/ppermute | solution.py:30
  9.1 12.1 %collective-permute-start.4 = (f32[256,128]{1,0:T(8,128)S(1)}, f32[256,128]{1,0:T(8,128)S(1)}, u32[]{:S(2)}, u32[]{:S(2)}) collective-permute-start(f32[256,128]{1,0:T(8,128)S(1)} %slice_select_fusion.panel_ref), channel_id=1, source_target_pairs={{0,1},{1,0},{2,3},{3,2},{4,5},{5,4},{6,7},{7,6},{8,9},{9,8},{10,11... | collective-permute-start | bytes 393224 | tf_op jit(solution)/shard_map/ppermute | solution.py:30
  15.4 5.8 %collective-permute-start.3 = (f32[192,128]{1,0:T(8,128)S(1)}, f32[192,128]{1,0:T(8,128)S(1)}, u32[]{:S(2)}, u32[]{:S(2)}) collective-permute-start(f32[192,128]{1,0:T(8,128)S(1)} %pad_maximum_fusion.5), channel_id=1, source_target_pairs={{0,56},{1,57},{4,60},{5,61},{10,50},{11,51},{14,54},{15,55},{16,40... | collective-permute-start | bytes 294920 | tf_op jit(solution)/shard_map/ppermute | solution.py:30
  21.2 4.5 %collective-permute-start.5 = (f32[192,128]{1,0:T(8,128)S(1)}, f32[192,128]{1,0:T(8,128)S(1)}, u32[]{:S(2)}, u32[]{:S(2)}) collective-permute-start(f32[192,128]{1,0:T(8,128)S(1)} %pad_maximum_fusion.6), channel_id=1, source_target_pairs={{0,16},{1,17},{2,18},{3,19},{4,20},{5,21},{6,22},{7,23},{8,24},{9,... | collective-permute-start | bytes 294920 | tf_op jit(solution)/shard_map/ppermute | solution.py:30
  25.7 12.5 %copy-start.2 = (f32[256,4096]{1,0:T(8,128)S(1)}, f32[256,4096]{1,0:T(8,128)}, u32[]{:S(2)}) copy-start(f32[256,4096]{1,0:T(8,128)} %a_ref.1) | copy-start | bytes 12582916
  25.7 4.7 %collective-permute-start.6 = (f32[320,128]{1,0:T(8,128)S(1)}, f32[320,128]{1,0:T(8,128)S(1)}, u32[]{:S(2)}, u32[]{:S(2)}) collective-permute-start(f32[320,128]{1,0:T(8,128)S(1)} %pad_maximum_fusion.3), channel_id=1, source_target_pairs={{0,8},{1,9},{2,10},{3,11},{4,12},{5,13},{6,14},{7,15},{8,0},{9,1},... | collective-permute-start | bytes 491528 | tf_op jit(solution)/shard_map/ppermute | solution.py:30
  27.2 13.4 %collective-permute-start.9 = (f32[256,128]{1,0:T(8,128)S(1)}, f32[256,128]{1,0:T(8,128)S(1)}, u32[]{:S(2)}, u32[]{:S(2)}) collective-permute-start(f32[256,128]{1,0:T(8,128)S(1)} %shard_map.18), channel_id=1, source_target_pairs={{0,3},{1,2},{2,1},{3,0},{4,7},{5,6},{6,5},{7,4},{8,11},{9,10},{10,... | collective-permute-start | bytes 393224 | tf_op jit(solution)/shard_map/ppermute | solution.py:30
  30.5 10.1 %collective-permute-start.8 = (f32[576,128]{1,0:T(8,128)S(1)}, f32[576,128]{1,0:T(8,128)S(1)}, u32[]{:S(2)}, u32[]{:S(2)}) collective-permute-start(f32[576,128]{1,0:T(8,128)S(1)} %pad_maximum_fusion), channel_id=1, source_target_pairs={{0,192},{1,193},{2,194},{3,195},{4,196},{5,197},{6,198},{7,199},{8... | collective-permute-start | bytes 884744 | tf_op jit(solution)/shard_map/ppermute | solution.py:30
  33.1 7.5 %collective-permute-start.7 = (f32[576,128]{1,0:T(8,128)S(1)}, f32[576,128]{1,0:T(8,128)S(1)}, u32[]{:S(2)}, u32[]{:S(2)}) collective-permute-start(f32[576,128]{1,0:T(8,128)S(1)} %pad_maximum_fusion), channel_id=1, source_target_pairs={{0,64},{1,65},{2,66},{3,67},{4,68},{5,69},{6,70},{7,71},{8,72},{9,... | collective-permute-start | bytes 884744 | tf_op jit(solution)/shard_map/ppermute | solution.py:30
  33.1 7.5 %collective-permute-start.10 = (f32[512,128]{1,0:T(8,128)S(1)}, f32[512,128]{1,0:T(8,128)S(1)}, u32[]{:S(2)}, u32[]{:S(2)}) collective-permute-start(f32[512,128]{1,0:T(8,128)S(1)} %pad_maximum_fusion.2.refs_2_), channel_id=1, source_target_pairs={{0,4},{1,5},{2,6},{3,7},{4,0},{5,1},{6,2},{7,3},{8,12},{9,13},{10,... | collective-permute-start | bytes 786440 | tf_op jit(solution)/shard_map/ppermute | solution.py:30
  38.5 2.0 %copy-start = (f32[256,4096]{1,0:T(8,128)}, f32[256,4096]{1,0:T(8,128)S(1)}, u32[]{:S(2)}) copy-start(f32[256,4096]{1,0:T(8,128)S(1)} %shard_map.19.refs_0_) | copy-start | bytes 12582916
  40.7 9.8 %collective-permute-start.13 = (f32[256,128]{1,0:T(8,128)S(1)}, f32[256,128]{1,0:T(8,128)S(1)}, u32[]{:S(2)}, u32[]{:S(2)}) collective-permute-start(f32[256,128]{1,0:T(8,128)S(1)} %slice.77), channel_id=1, source_target_pairs={{0,192},{1,193},{2,194},{3,195},{4,196},{5,197},{6,198},{7,199},{8... | collective-permute-start | bytes 393224 | tf_op jit(solution)/shard_map/ppermute | solution.py:30
  41.6 6.2 %copy-start.1 = (f32[256,4096]{1,0:T(8,128)S(1)}, f32[256,4096]{1,0:T(8,128)}, u32[]{:S(2)}) copy-start(f32[256,4096]{1,0:T(8,128)} %copy-done) | copy-start | bytes 12582916
  41.6 8.8 %collective-permute-start.12 = (f32[320,128]{1,0:T(8,128)S(1)}, f32[320,128]{1,0:T(8,128)S(1)}, u32[]{:S(2)}, u32[]{:S(2)}) collective-permute-start(f32[320,128]{1,0:T(8,128)S(1)} %pad_maximum_fusion.4), channel_id=1, source_target_pairs={{0,64},{1,65},{2,66},{3,67},{4,68},{5,69},{6,70},{7,71},{8,72},{9,... | collective-permute-start | bytes 491528 | tf_op jit(solution)/shard_map/ppermute | solution.py:30
  42.4 5.1 %collective-permute-start.14 = (f32[512,128]{1,0:T(8,128)S(1)}, f32[512,128]{1,0:T(8,128)S(1)}, u32[]{:S(2)}, u32[]{:S(2)}) collective-permute-start(f32[512,128]{1,0:T(8,128)S(1)} %slice.78), channel_id=1, source_target_pairs={{0,4},{1,5},{2,6},{3,7},{4,0},{5,1},{6,2},{7,3},{8,12},{9,13},{10,... | collective-permute-start | bytes 786440 | tf_op jit(solution)/shard_map/ppermute | solution.py:30
  46.3 1.5 %collective-permute-start.11 = (f32[512,128]{1,0:T(8,128)S(1)}, f32[512,128]{1,0:T(8,128)S(1)}, u32[]{:S(2)}, u32[]{:S(2)}) collective-permute-start(f32[512,128]{1,0:T(8,128)S(1)} %slice.74), channel_id=1, source_target_pairs={{0,4},{1,5},{2,6},{3,7},{4,0},{5,1},{6,2},{7,3},{8,12},{9,13},{10,... | collective-permute-start | bytes 786440 | tf_op jit(solution)/shard_map/ppermute | solution.py:30
  50.5 2.9 %collective-permute-start.15 = (f32[576,128]{1,0:T(8,128)S(1)}, f32[576,128]{1,0:T(8,128)S(1)}, u32[]{:S(2)}, u32[]{:S(2)}) collective-permute-start(f32[576,128]{1,0:T(8,128)S(1)} %pad_maximum_fusion.1.refs_6_), channel_id=1, source_target_pairs={{0,4},{1,5},{2,6},{3,7},{4,0},{5,1},{6,2},{7,3},{8,12},{9,13},{10,... | collective-permute-start | bytes 884744 | tf_op jit(solution)/shard_map/ppermute | solution.py:30

commit v5 on v4

--- a/solution.py
+++ b/solution.py
@@ -352,7 +352,8 @@
         lambda X, Y, Z, C: (X ^ 1, Y, Z, C),
     )
     far_b = move(near_a[2 * NB : 4 * NB], lambda X, Y, Z, C: (X ^ 3, Y, Z, C))
-    near_a_o, near_b_o = move(near_a[: 4 * NB], other), move(near_b[: 4 * NB], other)
+    near_o = move(jnp.concatenate([near_a[: 4 * NB], near_b[: 4 * NB]]), other)
+    near_a_o, near_b_o = near_o[: 4 * NB], near_o[4 * NB :]
     out = update((1, 3), staged, rows, [near_a, near_a_o, near_b, near_b_o])
     far_a, far_b, out = lax.optimization_barrier((far_a, far_b, out))
     seed = jnp.where(x == 1, near_a[4 * NB :], seed)

time: 55.8 us -> 57.1 us (1.023)
  waiting for transfers between devices: 8.45 us -> 9.74 us
  local copies, waits for them, and re-layouts: 2.13 us -> 2.79 us
  starting transfers between devices: 36.7 us -> 36.1 us
    ppermute x16 -> x15, waiting for transfers between devices: 8.45 us -> 9.74 us  [move(): return lax.ppermute(block, AXES, pairs)]
    unnamed x6, local copies, waits for them, and re-layouts: 2.02 us -> 2.65 us
    ppermute x16 -> x15, starting transfers between devices: 36.7 us -> 36.1 us  [move(): return lax.ppermute(block, AXES, pairs)]
  transfers between devices with their start and end apart: 16 -> 15, of which waited for: 6 -> 6; matrix products, arithmetic and copies ran while one was open for 0% -> 0% of each run, Pallas kernels for 8% -> 8%
where the time goes in v5:
time: 57.1 us; the launch traced here: 56.9 us
  starting transfers between devices  36.1 us (63%)
  waiting for transfers between devices  9.74 us (17%)
  Pallas kernels  6.62 us (12%)
  local copies, waits for them, and re-layouts  2.79 us (5%)
  other arithmetic  1.21 us (2%)
    ppermute x15, starting transfers between devices, move(): return lax.ppermute(block, AXES, pairs)  36.1 us
    ppermute x15, waiting for transfers between devices, move(): return lax.ppermute(block, AXES, pairs)  9.74 us
    pallas_call x3, Pallas kernels, update(): pl.pallas_call(kernel, out_shape=jax.ShapeDtypeStruct(matrix.shape, jnp.f...  6.26 us
    unnamed x6, local copies, waits for them, and re-layouts  2.65 us
  transfers between devices with their start and end apart: 15, of which 6 were waited for; matrix products, arithmetic and copies ran while one was open for 0% of the time, Pallas kernels for 8%

profile of v5, /device:TPU:1, one launch (start us, length us, event | category | flops | bytes accessed | tf_op | source)
XLA Modules:
  0.0 56.9 jit_solution(3517701216023971485)
XLA Ops:
  0.0 1.0 %slice_select_fusion.panel_ref = f32[256,128]{1,0:T(8,128)S(1)} fusion(f32[256,4096]{1,0:T(8,128)} %a_ref.1, pred[256]{0:T(512)(128)(4,1)S(1)} %compare_or_fusion), kind=kLoop, calls=%fused_computation.6 | loop fusion | flops 32768 | bytes 262400 | tf_op jit(solution)/shard_map/jit(_where)/select_n | solution.py:272
  1.0 4.6 %collective-permute-start.1 = (f32[128,128]{1,0:T(8,128)S(1)}, f32[128,128]{1,0:T(8,128)S(1)}, u32[]{:S(2)}, u32[]{:S(2)}) collective-permute-start(f32[128,128]{1,0:T(8,128)S(1)} %get-tuple-element.35), channel_id=1, source_target_pairs={{0,0},{4,1},{8,10},{12,11},{16,16},{20,17},{24,26},{28,27},{32,32}... | collective-permute-start | bytes 196616 | tf_op jit(solution)/shard_map/ppermute | solution.py:30
  5.6 1.9 %collective-permute-start = (f32[128,128]{1,0:T(8,128)S(1)}, f32[128,128]{1,0:T(8,128)S(1)}, u32[]{:S(2)}, u32[]{:S(2)}) collective-permute-start(f32[128,128]{1,0:T(8,128)S(1)} %get-tuple-element.36.a_ref), channel_id=1, source_target_pairs={{0,4},{4,5},{8,14},{12,15},{16,20},{20,21},{24,30},{28,31},{32,36}... | collective-permute-start | bytes 196616 | tf_op jit(solution)/shard_map/ppermute | solution.py:30
  7.6 1.3 %collective-permute-done = f32[128,128]{1,0:T(8,128)S(1)} collective-permute-done((f32[128,128]{1,0:T(8,128)S(1)}, f32[128,128]{1,0:T(8,128)S(1)}, u32[]{:S(2)}, u32[]{:S(2)}) %collective-permute-start) | collective-permute-done | bytes 65568 | tf_op jit(solution)/shard_map/ppermute | solution.py:30
  9.1 6.3 %collective-permute-start.4 = (f32[256,128]{1,0:T(8,128)S(1)}, f32[256,128]{1,0:T(8,128)S(1)}, u32[]{:S(2)}, u32[]{:S(2)}) collective-permute-start(f32[256,128]{1,0:T(8,128)S(1)} %slice_select_fusion.panel_ref), channel_id=1, source_target_pairs={{0,1},{1,0},{2,3},{3,2},{4,5},{5,4},{6,7},{7,6},{8,9},{9,8},{10,11... | collective-permute-start | bytes 393224 | tf_op jit(solution)/shard_map/ppermute | solution.py:30
  15.4 4.0 %collective-permute-start.3 = (f32[192,128]{1,0:T(8,128)S(1)}, f32[192,128]{1,0:T(8,128)S(1)}, u32[]{:S(2)}, u32[]{:S(2)}) collective-permute-start(f32[192,128]{1,0:T(8,128)S(1)} %pad_maximum_fusion.6), channel_id=1, source_target_pairs={{0,56},{1,57},{4,60},{5,61},{10,50},{11,51},{14,54},{15,55},{16,40... | collective-permute-start | bytes 294920 | tf_op jit(solution)/shard_map/ppermute | solution.py:30
  19.4 1.7 %collective-permute-done.3 = f32[192,128]{1,0:T(8,128)S(1)} collective-permute-done((f32[192,128]{1,0:T(8,128)S(1)}, f32[192,128]{1,0:T(8,128)S(1)}, u32[]{:S(2)}, u32[]{:S(2)}) %collective-permute-start.3) | collective-permute-done | bytes 98336 | tf_op jit(solution)/shard_map/ppermute | solution.py:30
  21.2 2.2 %collective-permute-start.5 = (f32[192,128]{1,0:T(8,128)S(1)}, f32[192,128]{1,0:T(8,128)S(1)}, u32[]{:S(2)}, u32[]{:S(2)}) collective-permute-start(f32[192,128]{1,0:T(8,128)S(1)} %pad_maximum_fusion.7), channel_id=1, source_target_pairs={{0,16},{1,17},{2,18},{3,19},{4,20},{5,21},{6,22},{7,23},{8,24},{9,... | collective-permute-start | bytes 294920 | tf_op jit(solution)/shard_map/ppermute | solution.py:30
  23.4 2.3 %collective-permute-done.5 = f32[192,128]{1,0:T(8,128)S(1)} collective-permute-done((f32[192,128]{1,0:T(8,128)S(1)}, f32[192,128]{1,0:T(8,128)S(1)}, u32[]{:S(2)}, u32[]{:S(2)}) %collective-permute-start.5) | collective-permute-done | bytes 98336 | tf_op jit(solution)/shard_map/ppermute | solution.py:30
  25.7 1.4 %collective-permute-start.6 = (f32[320,128]{1,0:T(8,128)S(1)}, f32[320,128]{1,0:T(8,128)S(1)}, u32[]{:S(2)}, u32[]{:S(2)}) collective-permute-start(f32[320,128]{1,0:T(8,128)S(1)} %pad_maximum_fusion.4), channel_id=1, source_target_pairs={{0,8},{1,9},{2,10},{3,11},{4,12},{5,13},{6,14},{7,15},{8,0},{9,1},... | collective-permute-start | bytes 491528 | tf_op jit(solution)/shard_map/ppermute | solution.py:30
  27.2 1.4 %collective-permute-start.9 = (f32[256,128]{1,0:T(8,128)S(1)}, f32[256,128]{1,0:T(8,128)S(1)}, u32[]{:S(2)}, u32[]{:S(2)}) collective-permute-start(f32[256,128]{1,0:T(8,128)S(1)} %shard_map.18), channel_id=1, source_target_pairs={{0,3},{1,2},{2,1},{3,0},{4,7},{5,6},{6,5},{7,4},{8,11},{9,10},{10,... | collective-permute-start | bytes 393224 | tf_op jit(solution)/shard_map/ppermute | solution.py:30
  28.6 1.9 %collective-permute-done.6 = f32[320,128]{1,0:T(8,128)S(1)} collective-permute-done((f32[320,128]{1,0:T(8,128)S(1)}, f32[320,128]{1,0:T(8,128)S(1)}, u32[]{:S(2)}, u32[]{:S(2)}) %collective-permute-start.6) | collective-permute-done | bytes 163872 | tf_op jit(solution)/shard_map/ppermute | solution.py:30
  30.5 2.6 %collective-permute-start.8 = (f32[576,128]{1,0:T(8,128)S(1)}, f32[576,128]{1,0:T(8,128)S(1)}, u32[]{:S(2)}, u32[]{:S(2)}) collective-permute-start(f32[576,128]{1,0:T(8,128)S(1)} %pad_maximum_fusion.1), channel_id=1, source_target_pairs={{0,192},{1,193},{2,194},{3,195},{4,196},{5,197},{6,198},{7,199},{8... | collective-permute-start | bytes 884744 | tf_op jit(solution)/shard_map/ppermute | solution.py:30
  33.1 5.2 %collective-permute-start.10 = (f32[512,128]{1,0:T(8,128)S(1)}, f32[512,128]{1,0:T(8,128)S(1)}, u32[]{:S(2)}, u32[]{:S(2)}) collective-permute-start(f32[512,128]{1,0:T(8,128)S(1)} %pad_maximum_fusion.3.refs_2_), channel_id=1, source_target_pairs={{0,4},{1,5},{2,6},{3,7},{4,0},{5,1},{6,2},{7,3},{8,12},{9,13},{10,... | collective-permute-start | bytes 786440 | tf_op jit(solution)/shard_map/ppermute | solution.py:30
  38.5 2.0 %copy-done = f32[256,4096]{1,0:T(8,128)} copy-done((f32[256,4096]{1,0:T(8,128)}, f32[256,4096]{1,0:T(8,128)S(1)}, u32[]{:S(2)}) %copy-start) | copy-done | bytes 4194328
  40.7 0.9 %collective-permute-start.13 = (f32[256,128]{1,0:T(8,128)S(1)}, f32[256,128]{1,0:T(8,128)S(1)}, u32[]{:S(2)}, u32[]{:S(2)}) collective-permute-start(f32[256,128]{1,0:T(8,128)S(1)} %slice.85), channel_id=1, source_target_pairs={{0,192},{1,193},{2,194},{3,195},{4,196},{5,197},{6,198},{7,199},{8... | collective-permute-start | bytes 393224 | tf_op jit(solution)/shard_map/ppermute | solution.py:30
  41.7 4.6 %collective-permute-start.11 = (f32[1024,128]{1,0:T(8,128)S(1)}, f32[1024,128]{1,0:T(8,128)S(1)}, u32[]{:S(2)}, u32[]{:S(2)}) collective-permute-start(f32[1024,128]{1,0:T(8,128)S(1)} %pad_maximum_fusion), channel_id=1, source_target_pairs={{0,4},{1,5},{2,6},{3,7},{4,0},{5,1},{6,2},{7,3},{8,12},{9,13},{10,... | collective-permute-start | bytes 1572872 | tf_op jit(solution)/shard_map/ppermute | solution.py:30
  46.4 1.4 %collective-permute-done.11 = f32[1024,128]{1,0:T(8,128)S(1)} collective-permute-done((f32[1024,128]{1,0:T(8,128)S(1)}, f32[1024,128]{1,0:T(8,128)S(1)}, u32[]{:S(2)}, u32[]{:S(2)}) %collective-permute-start.11) | collective-permute-done | bytes 524320 | tf_op jit(solution)/shard_map/ppermute | solution.py:30
  47.8 0.6 %copy-done.1 = f32[256,4096]{1,0:T(8,128)S(1)} copy-done((f32[256,4096]{1,0:T(8,128)S(1)}, f32[256,4096]{1,0:T(8,128)}, u32[]{:S(2)}) %copy-start.1) | copy-done | bytes 4194328
  48.5 2.6 %shard_map.21.refs_4_ = f32[256,4096]{1,0:T(8,128)} custom-call(f32[256,4096]{1,0:T(8,128)S(1)} %copy-done.1, f32[256,128]{1,0:T(8,128)S(1)} %shard_map.20.refs_1_, f32[576,128]{1,0:T(8,128)S(1)} %collective-permute-done.7.refs_2_.refs_4_, f32[512,128]{1,0:T(8,128)S(1)} %get-tuple-element.34.refs_3_.refs_5_, ...), custom_call_target="tpu_custom_call" | custom-call | flops 536870912 | bytes 4194304 | tf_op jit(solution)/shard_map/pallas_call | solution.py:251
  51.0 1.1 %collective-permute-done.12 = f32[320,128]{1,0:T(8,128)S(1)} collective-permute-done((f32[320,128]{1,0:T(8,128)S(1)}, f32[320,128]{1,0:T(8,128)S(1)}, u32[]{:S(2)}, u32[]{:S(2)}) %collective-permute-start.12) | collective-permute-done | bytes 163872 | tf_op jit(solution)/shard_map/ppermute | solution.py:30
  52.2 0.9 %collective-permute-start.14 = (f32[576,128]{1,0:T(8,128)S(1)}, f32[576,128]{1,0:T(8,128)S(1)}, u32[]{:S(2)}, u32[]{:S(2)}) collective-permute-start(f32[576,128]{1,0:T(8,128)S(1)} %pad_maximum_fusion.2.refs_6_), channel_id=1, source_target_pairs={{0,4},{1,5},{2,6},{3,7},{4,0},{5,1},{6,2},{7,3},{8,12},{9,13},{10,... | collective-permute-start | bytes 884744 | tf_op jit(solution)/shard_map/ppermute | solution.py:30
  53.1 1.7 %shard_map.22.refs_12_ = f32[256,4096]{1,0:T(8,128)} custom-call(f32[256,4096]{1,0:T(8,128)S(1)} %copy-done.1, f32[256,128]{1,0:T(8,128)S(1)} %shard_map.20.refs_1_, f32[512,128]{1,0:T(8,128)S(1)} %pad_maximum_fusion.3.refs_2_, f32[512,128]{1,0:T(8,128)S(1)} %collective-permute-done.10.refs_3_, ...), custom_call_target="tpu_custom_call", output_to_operand_aliasing={{}: (4, {})} | custom-call | flops 268435456 | bytes 2097152 | tf_op jit(solution)/shard_map/pallas_call | solution.py:251
  54.9 2.0 %shard_map.23 = f32[256,4096]{1,0:T(8,128)} custom-call(f32[256,4096]{1,0:T(8,128)S(1)} %copy-done.1, f32[256,128]{1,0:T(8,128)S(1)} %shard_map.20.refs_1_, f32[512,128]{1,0:T(8,128)S(1)} %pad_maximum_fusion.3.refs_2_, f32[512,128]{1,0:T(8,128)S(1)} %collective-permute-done.10.refs_3_, ...), custom_call_target="tpu_custom_call", output_to_operand_aliasing={{}: (12, {})} | custom-call | flops 268435456 | bytes 2097152 | tf_op jit(solution)/shard_map/pallas_call | solution.py:251
  (49 shorter events, 1.0 us)
Async XLA Ops:
  1.0 6.5 %collective-permute-start.1 = (f32[128,128]{1,0:T(8,128)S(1)}, f32[128,128]{1,0:T(8,128)S(1)}, u32[]{:S(2)}, u32[]{:S(2)}) collective-permute-start(f32[128,128]{1,0:T(8,128)S(1)} %get-tuple-element.35), channel_id=1, source_target_pairs={{0,0},{4,1},{8,10},{12,11},{16,16},{20,17},{24,26},{28,27},{32,32}... | collective-permute-start | bytes 196616 | tf_op jit(solution)/shard_map/ppermute | solution.py:30
  5.6 3.2 %collective-permute-start = (f32[128,128]{1,0:T(8,128)S(1)}, f32[128,128]{1,0:T(8,128)S(1)}, u32[]{:S(2)}, u32[]{:S(2)}) collective-permute-start(f32[128,128]{1,0:T(8,128)S(1)} %get-tuple-element.36.a_ref), channel_id=1, source_target_pairs={{0,4},{4,5},{8,14},{12,15},{16,20},{20,21},{24,30},{28,31},{32,36}... | collective-permute-start | bytes 196616 | tf_op jit(solution)/shard_map/ppermute | solution.py:30
  8.9 6.4 %collective-permute-start.2 = (f32[64,128]{1,0:T(8,128)S(1)}, f32[64,128]{1,0:T(8,128)S(1)}, u32[]{:S(2)}, u32[]{:S(2)}) collective-permute-start(f32[64,128]{1,0:T(8,128)S(1)} %slice.73), channel_id=1, source_target_pairs={{0,4},{1,5},{2,6},{3,7},{4,0},{5,1},{6,2},{7,3},{8,12},{9,13},{10,... | collective-permute-start | bytes 98312 | tf_op jit(solution)/shard_map/ppermute | solution.py:30
  9.1 12.1 %collective-permute-start.4 = (f32[256,128]{1,0:T(8,128)S(1)}, f32[256,128]{1,0:T(8,128)S(1)}, u32[]{:S(2)}, u32[]{:S(2)}) collective-permute-start(f32[256,128]{1,0:T(8,128)S(1)} %slice_select_fusion.panel_ref), channel_id=1, source_target_pairs={{0,1},{1,0},{2,3},{3,2},{4,5},{5,4},{6,7},{7,6},{8,9},{9,8},{10,11... | collective-permute-start | bytes 393224 | tf_op jit(solution)/shard_map/ppermute | solution.py:30
  15.4 5.8 %collective-permute-start.3 = (f32[192,128]{1,0:T(8,128)S(1)}, f32[192,128]{1,0:T(8,128)S(1)}, u32[]{:S(2)}, u32[]{:S(2)}) collective-permute-start(f32[192,128]{1,0:T(8,128)S(1)} %pad_maximum_fusion.6), channel_id=1, source_target_pairs={{0,56},{1,57},{4,60},{5,61},{10,50},{11,51},{14,54},{15,55},{16,40... | collective-permute-start | bytes 294920 | tf_op jit(solution)/shard_map/ppermute | solution.py:30
  21.2 4.5 %collective-permute-start.5 = (f32[192,128]{1,0:T(8,128)S(1)}, f32[192,128]{1,0:T(8,128)S(1)}, u32[]{:S(2)}, u32[]{:S(2)}) collective-permute-start(f32[192,128]{1,0:T(8,128)S(1)} %pad_maximum_fusion.7), channel_id=1, source_target_pairs={{0,16},{1,17},{2,18},{3,19},{4,20},{5,21},{6,22},{7,23},{8,24},{9,... | collective-permute-start | bytes 294920 | tf_op jit(solution)/shard_map/ppermute | solution.py:30
  25.7 12.5 %copy-start.2 = (f32[256,4096]{1,0:T(8,128)S(1)}, f32[256,4096]{1,0:T(8,128)}, u32[]{:S(2)}) copy-start(f32[256,4096]{1,0:T(8,128)} %a_ref.1) | copy-start | bytes 12582916
  25.7 4.7 %collective-permute-start.6 = (f32[320,128]{1,0:T(8,128)S(1)}, f32[320,128]{1,0:T(8,128)S(1)}, u32[]{:S(2)}, u32[]{:S(2)}) collective-permute-start(f32[320,128]{1,0:T(8,128)S(1)} %pad_maximum_fusion.4), channel_id=1, source_target_pairs={{0,8},{1,9},{2,10},{3,11},{4,12},{5,13},{6,14},{7,15},{8,0},{9,1},... | collective-permute-start | bytes 491528 | tf_op jit(solution)/shard_map/ppermute | solution.py:30
  27.2 13.4 %collective-permute-start.9 = (f32[256,128]{1,0:T(8,128)S(1)}, f32[256,128]{1,0:T(8,128)S(1)}, u32[]{:S(2)}, u32[]{:S(2)}) collective-permute-start(f32[256,128]{1,0:T(8,128)S(1)} %shard_map.18), channel_id=1, source_target_pairs={{0,3},{1,2},{2,1},{3,0},{4,7},{5,6},{6,5},{7,4},{8,11},{9,10},{10,... | collective-permute-start | bytes 393224 | tf_op jit(solution)/shard_map/ppermute | solution.py:30
  30.5 10.1 %collective-permute-start.8 = (f32[576,128]{1,0:T(8,128)S(1)}, f32[576,128]{1,0:T(8,128)S(1)}, u32[]{:S(2)}, u32[]{:S(2)}) collective-permute-start(f32[576,128]{1,0:T(8,128)S(1)} %pad_maximum_fusion.1), channel_id=1, source_target_pairs={{0,192},{1,193},{2,194},{3,195},{4,196},{5,197},{6,198},{7,199},{8... | collective-permute-start | bytes 884744 | tf_op jit(solution)/shard_map/ppermute | solution.py:30
  33.1 7.5 %collective-permute-start.7 = (f32[576,128]{1,0:T(8,128)S(1)}, f32[576,128]{1,0:T(8,128)S(1)}, u32[]{:S(2)}, u32[]{:S(2)}) collective-permute-start(f32[576,128]{1,0:T(8,128)S(1)} %pad_maximum_fusion.1), channel_id=1, source_target_pairs={{0,64},{1,65},{2,66},{3,67},{4,68},{5,69},{6,70},{7,71},{8,72},{9,... | collective-permute-start | bytes 884744 | tf_op jit(solution)/shard_map/ppermute | solution.py:30
  33.1 7.5 %collective-permute-start.10 = (f32[512,128]{1,0:T(8,128)S(1)}, f32[512,128]{1,0:T(8,128)S(1)}, u32[]{:S(2)}, u32[]{:S(2)}) collective-permute-start(f32[512,128]{1,0:T(8,128)S(1)} %pad_maximum_fusion.3.refs_2_), channel_id=1, source_target_pairs={{0,4},{1,5},{2,6},{3,7},{4,0},{5,1},{6,2},{7,3},{8,12},{9,13},{10,... | collective-permute-start | bytes 786440 | tf_op jit(solution)/shard_map/ppermute | solution.py:30
  38.5 2.0 %copy-start = (f32[256,4096]{1,0:T(8,128)}, f32[256,4096]{1,0:T(8,128)S(1)}, u32[]{:S(2)}) copy-start(f32[256,4096]{1,0:T(8,128)S(1)} %shard_map.19.refs_0_) | copy-start | bytes 12582916
  40.7 10.4 %collective-permute-start.13 = (f32[256,128]{1,0:T(8,128)S(1)}, f32[256,128]{1,0:T(8,128)S(1)}, u32[]{:S(2)}, u32[]{:S(2)}) collective-permute-start(f32[256,128]{1,0:T(8,128)S(1)} %slice.85), channel_id=1, source_target_pairs={{0,192},{1,193},{2,194},{3,195},{4,196},{5,197},{6,198},{7,199},{8... | collective-permute-start | bytes 393224 | tf_op jit(solution)/shard_map/ppermute | solution.py:30
  41.7 6.1 %collective-permute-start.11 = (f32[1024,128]{1,0:T(8,128)S(1)}, f32[1024,128]{1,0:T(8,128)S(1)}, u32[]{:S(2)}, u32[]{:S(2)}) collective-permute-start(f32[1024,128]{1,0:T(8,128)S(1)} %pad_maximum_fusion), channel_id=1, source_target_pairs={{0,4},{1,5},{2,6},{3,7},{4,0},{5,1},{6,2},{7,3},{8,12},{9,13},{10,... | collective-permute-start | bytes 1572872 | tf_op jit(solution)/shard_map/ppermute | solution.py:30
  46.3 2.2 %copy-start.1 = (f32[256,4096]{1,0:T(8,128)S(1)}, f32[256,4096]{1,0:T(8,128)}, u32[]{:S(2)}) copy-start(f32[256,4096]{1,0:T(8,128)} %copy-done) | copy-start | bytes 12582916
  46.3 5.9 %collective-permute-start.12 = (f32[320,128]{1,0:T(8,128)S(1)}, f32[320,128]{1,0:T(8,128)S(1)}, u32[]{:S(2)}, u32[]{:S(2)}) collective-permute-start(f32[320,128]{1,0:T(8,128)S(1)} %pad_maximum_fusion.5), channel_id=1, source_target_pairs={{0,64},{1,65},{2,66},{3,67},{4,68},{5,69},{6,70},{7,71},{8,72},{9,... | collective-permute-start | bytes 491528 | tf_op jit(solution)/shard_map/ppermute | solution.py:30
  52.2 2.6 %collective-permute-start.14 = (f32[576,128]{1,0:T(8,128)S(1)}, f32[576,128]{1,0:T(8,128)S(1)}, u32[]{:S(2)}, u32[]{:S(2)}) collective-permute-start(f32[576,128]{1,0:T(8,128)S(1)} %pad_maximum_fusion.2.refs_6_), channel_id=1, source_target_pairs={{0,4},{1,5},{2,6},{3,7},{4,0},{5,1},{6,2},{7,3},{8,12},{9,13},{10,... | collective-permute-start | bytes 884744 | tf_op jit(solution)/shard_map/ppermute | solution.py:30
